TPU v7x, 256 devices: a whole 4x4x8 slice. The times are simulated.
256 devices in a mesh: ctx: 16 (over z_hi, y), ch: 16 (over x, z_lo, core).
Axes of the slice: x: 4, y: 4, z: 8 (z_hi: 4, z_lo: 2; z = z_hi * 2 + z_lo), core: 2. Of those that a mesh axis runs over, the one named last changes fastest.
Arguments:
- prefix_values: bfloat16 [4096, 4096], P('ctx', 'ch'), may hold values from -6 to 6
- inner_gate: bfloat16 [4096, 4096], P('ctx', 'ch'), may hold values from -6 to 6
- outer_gate: bfloat16 [4096, 4096], P('ctx', 'ch'), may hold values from -6 to 6
- inner_filter: bfloat16 [4096, 4096], P('ctx', 'ch'), may hold values from -0.09375 to 0.09375
- outer_filter: bfloat16 [4096, 4096], P('ctx', 'ch'), may hold values from -0.09375 to 0.09375
- response_values: bfloat16 [16, 1024, 4096], P('ctx', None, 'ch'), may hold values from -6 to 6
- response_inner: bfloat16 [16, 1024, 4096], P('ctx', None, 'ch'), may hold values from -6 to 6
- response_outer: bfloat16 [16, 1024, 4096], P('ctx', None, 'ch'), may hold values from -6 to 6
- lengths: int32 [16], P('ctx'), may hold values from 1 to 1024, 12288 in all
- readout: float32 [4096], P('ch'), may hold values from -1 to 1
Outputs:
- prefix_output: bfloat16 [4096, 4096], P('ctx', 'ch')
- response_output: bfloat16 [16, 1024, 4096], P('ctx', None, 'ch')
- scores: float32 [16], P('ctx')
Inputs may be any that keep to these rules, and one draw needn't show every extreme that they name: `lengths`: a response's valid tokens are its first ones; some response has all 1024.
All inputs are finite; a program needn't handle non-finite values. No bound on the sum of `lengths` on one device may be relied on, other than what follows from the above.
Results may differ from a plain program's by a relative error of at most 0.0049.
Values may be sent and summed in bfloat16 or wider, within the bound.
A program may use at most 128 MiB of HBM per device.

v0:
```python
import math

import jax
import jax.numpy as jnp
from jax import lax
from jax.sharding import PartitionSpec as P


def contract(form, left, right):
    return jnp.einsum(form, left, right, precision=lax.Precision.HIGH)


def phase_table(row_count, col_count, length):
    products = (
        jnp.arange(row_count, dtype=jnp.int32)[:, None]
        * jnp.arange(col_count, dtype=jnp.int32)[None, :]
        % length
    )
    angles = products.astype(jnp.float32) * (2.0 * math.pi / length)
    return (jnp.cos(angles), jnp.sin(angles))


def forward_spectrum(signal, factor):
    half_length, columns = signal.shape
    length = 2 * half_length
    second = length // factor
    folded = signal.reshape(factor // 2, second, columns).transpose(1, 2, 0)
    cos_first, sin_first = phase_table(factor // 2, factor, factor)
    part_real = contract("bca,ak->bck", folded, cos_first)
    part_imag = -contract("bca,ak->bck", folded, sin_first)
    cos_twist, sin_twist = phase_table(second, factor, length)
    cos_twist = cos_twist[:, None, :]
    sin_twist = sin_twist[:, None, :]
    twist_real = part_real * cos_twist + part_imag * sin_twist
    twist_imag = part_imag * cos_twist - part_real * sin_twist
    cos_second, sin_second = phase_table(second, second, second)
    spectrum_real = contract("bck,bm->mck", twist_real, cos_second) + contract(
        "bck,bm->mck", twist_imag, sin_second
    )
    spectrum_imag = contract("bck,bm->mck", twist_imag, cos_second) - contract(
        "bck,bm->mck", twist_real, sin_second
    )
    return (spectrum_real, spectrum_imag)


def inverse_signal(spectrum_real, spectrum_imag, factor):
    second, columns, _ = spectrum_real.shape
    length = factor * second
    cos_second, sin_second = phase_table(second, second, second)
    mixed_real = contract("mck,mb->bck", spectrum_real, cos_second) - contract(
        "mck,mb->bck", spectrum_imag, sin_second
    )
    mixed_imag = contract("mck,mb->bck", spectrum_imag, cos_second) + contract(
        "mck,mb->bck", spectrum_real, sin_second
    )
    cos_twist, sin_twist = phase_table(second, factor, length)
    cos_twist = cos_twist[:, None, :]
    sin_twist = sin_twist[:, None, :]
    twist_real = mixed_real * cos_twist - mixed_imag * sin_twist
    twist_imag = mixed_imag * cos_twist + mixed_real * sin_twist
    cos_first, sin_first = phase_table(factor, factor, factor)
    values = contract("bck,ka->bca", twist_real, cos_first) - contract(
        "bck,ka->bca", twist_imag, sin_first
    )
    return values.transpose(2, 0, 1).reshape(length, columns) / length


def long_convolution(signal, filter_taps, factor):
    signal_real, signal_imag = forward_spectrum(signal.astype(jnp.float32), factor)
    taps_real, taps_imag = forward_spectrum(filter_taps.astype(jnp.float32), factor)
    product_real = signal_real * taps_real - signal_imag * taps_imag
    product_imag = signal_real * taps_imag + signal_imag * taps_real
    return inverse_signal(product_real, product_imag, factor)


def response_convolution(signals, head_taps):
    taps_real, taps_imag = forward_spectrum(head_taps, 128)

    def single(signal):
        signal_real, signal_imag = forward_spectrum(signal.astype(jnp.float32), 128)
        product_real = signal_real * taps_real - signal_imag * taps_imag
        product_imag = signal_real * taps_imag + signal_imag * taps_real
        return inverse_signal(product_real, product_imag, 128)[: signal.shape[0]]

    return jax.vmap(single)(signals)


def spread_channels(signal, filter_taps):
    return (
        lax.all_to_all(signal, "ctx", split_axis=1, concat_axis=0, tiled=True),
        lax.all_to_all(filter_taps, "ctx", split_axis=1, concat_axis=0, tiled=True),
    )


def return_tokens(values):
    return lax.all_to_all(values, "ctx", split_axis=0, concat_axis=1, tiled=True)


def collect_tails(full_conv, filter_cols, resp_length):
    prefix_length = filter_cols.shape[0]
    tail_rows = full_conv[prefix_length : prefix_length + resp_length]
    head_rows = filter_cols[:resp_length].astype(jnp.float32)
    return (
        lax.all_gather(tail_rows, "ctx", axis=1, tiled=True),
        lax.all_gather(head_rows, "ctx", axis=1, tiled=True),
    )


def per_device(
    prefix_values,
    inner_gate,
    outer_gate,
    inner_filter,
    outer_filter,
    response_values,
    response_inner,
    response_outer,
    lengths,
    readout,
):
    resp_length = response_values.shape[1]
    signal_cols, inner_cols = spread_channels(prefix_values, inner_filter)
    prefix_length = signal_cols.shape[0]
    full_one = long_convolution(signal_cols, inner_cols, 256)
    gathered_one = collect_tails(full_one, inner_cols, resp_length)
    gated_one = (inner_gate.astype(jnp.float32) * return_tokens(full_one[:prefix_length])).astype(
        jnp.bfloat16
    )
    gated_cols, outer_cols = spread_channels(gated_one, outer_filter)
    full_two = long_convolution(gated_cols, outer_cols, 256)
    gathered_two = collect_tails(full_two, outer_cols, resp_length)
    prefix_output = (
        outer_gate.astype(jnp.float32) * return_tokens(full_two[:prefix_length])
    ).astype(jnp.bfloat16)
    tail_one, head_one = gathered_one
    own_one = response_convolution(response_values, head_one)
    response_gated = (response_inner.astype(jnp.float32) * (tail_one[None] + own_one)).astype(
        jnp.bfloat16
    )
    tail_two, head_two = gathered_two
    own_two = response_convolution(response_gated, head_two)
    in_range = jnp.arange(resp_length, dtype=jnp.int32)[None, :] < lengths[:, None]
    ungated = response_outer.astype(jnp.float32) * (tail_two[None] + own_two)
    response_output = jnp.where(in_range[:, :, None], ungated, 0.0).astype(jnp.bfloat16)
    partial_value = jnp.sum(response_output.astype(jnp.float32) * readout[None, None, :], axis=2)
    projection = lax.psum(partial_value, "ch")
    squares = jnp.where(in_range, projection * projection, 0.0)
    scores = jnp.sum(squares, axis=1) / lengths.astype(jnp.float32)
    return (prefix_output, response_output, scores)


def solution(mesh):
    in_specs = (
        P("ctx", "ch"),
        P("ctx", "ch"),
        P("ctx", "ch"),
        P("ctx", "ch"),
        P("ctx", "ch"),
        P("ctx", None, "ch"),
        P("ctx", None, "ch"),
        P("ctx", None, "ch"),
        P("ctx"),
        P("ch"),
    )
    out_specs = (P("ctx", "ch"), P("ctx", None, "ch"), P("ctx"))
    return jax.shard_map(
        per_device, mesh=mesh, in_specs=in_specs, out_specs=out_specs, check_vma=False
    )
```

profile of v0, /device:TPU:1, one launch (start us, length us, event | category | flops | bytes accessed | tf_op | source)
XLA Modules:
  0.0 342.1 jit_solution(7948102361389554211)
XLA Ops:
  7.2 1.8 copy.265
  9.0 11.7 %all-to-all-start.1 = ((bf16[256,16,16]{0,2,1:T(8,128)(2,1)}), bf16[256,16,16]{0,2,1:T(8,128)(2,1)S(1)}, u32[]{:S(2)}, u32[]{:S(2)}) async-start(bf16[256,16,16]{0,2,1:T(8,128)(2,1)} %bitcast.10), calls=%async_computation.1 | async-start | bytes 262144 | tf_op jit(solution)/shard_map/all_to_all | solution.py:91
  20.9 1.7 copy.275
  22.5 1.7 copy.262
  24.2 2.0 copy.282
  30.4 9.1 %all-to-all-start = ((bf16[256,16,16]{0,2,1:T(8,128)(2,1)}), bf16[256,16,16]{0,2,1:T(8,128)(2,1)S(1)}, u32[]{:S(2)}, u32[]{:S(2)}) async-start(bf16[256,16,16]{0,2,1:T(8,128)(2,1)} %bitcast.3), calls=%async_computation | async-start | bytes 262144 | tf_op jit(solution)/shard_map/all_to_all | solution.py:90
  43.0 5.6 %all-to-all-done = bf16[256,16,16]{0,2,1:T(8,128)(2,1)S(1)} async-done(((bf16[256,16,16]{0,2,1:T(8,128)(2,1)}), bf16[256,16,16]{0,2,1:T(8,128)(2,1)S(1)}, u32[]{:S(2)}, u32[]{:S(2)}) %all-to-all-start) | async-done | bytes 131104 | tf_op jit(solution)/shard_map/all_to_all | solution.py:90
  48.7 3.5 %all-to-all-start.4 = ((bf16[256,16,16]{0,2,1:T(8,128)(2,1)}), bf16[256,16,16]{0,2,1:T(8,128)(2,1)S(1)}, u32[]{:S(2)}, u32[]{:S(2)}) async-start(bf16[256,16,16]{0,2,1:T(8,128)(2,1)} %bitcast.22), calls=%async_computation.4 | async-start | bytes 262144 | tf_op jit(solution)/shard_map/all_to_all | solution.py:91
  55.3 6.1 %all-to-all-done.4 = bf16[256,16,16]{0,2,1:T(8,128)(2,1)S(1)} async-done(((bf16[256,16,16]{0,2,1:T(8,128)(2,1)}), bf16[256,16,16]{0,2,1:T(8,128)(2,1)S(1)}, u32[]{:S(2)}, u32[]{:S(2)}) %all-to-all-start.4) | async-done | bytes 131104 | tf_op jit(solution)/shard_map/all_to_all | solution.py:91
  69.6 2.1 multiply_subtract_fusion.6
  79.3 3.5 %all-to-all-start.2 = ((f32[16,256,16]{1,2,0:T(8,128)}), f32[16,256,16]{1,2,0:T(8,128)S(1)}, u32[]{:S(2)}, u32[]{:S(2)}) async-start(f32[16,256,16]{1,2,0:T(8,128)} %copy.269), calls=%async_computation.2 | async-start | bytes 524288 | tf_op jit(solution)/shard_map/all_to_all | solution.py:96
  86.2 1.7 fusion.26
  90.9 8.8 %all-to-all-done.2 = f32[16,256,16]{1,2,0:T(8,128)S(1)} async-done(((f32[16,256,16]{1,2,0:T(8,128)}), f32[16,256,16]{1,2,0:T(8,128)S(1)}, u32[]{:S(2)}, u32[]{:S(2)}) %all-to-all-start.2) | async-done | bytes 262176 | tf_op jit(solution)/shard_map/all_to_all | solution.py:96
  101.3 3.6 %all-to-all-start.3 = ((bf16[256,16,16]{0,2,1:T(8,128)(2,1)}), bf16[256,16,16]{0,2,1:T(8,128)(2,1)S(1)}, u32[]{:S(2)}, u32[]{:S(2)}) async-start(bf16[256,16,16]{0,2,1:T(8,128)(2,1)} %bitcast.390), calls=%async_computation.3 | async-start | bytes 262144 | tf_op jit(solution)/shard_map/all_to_all | solution.py:90
  104.9 2.3 convolution_subtract_fusion.5
  107.2 6.9 %all-to-all-done.3 = bf16[256,16,16]{0,2,1:T(8,128)(2,1)S(1)} async-done(((bf16[256,16,16]{0,2,1:T(8,128)(2,1)}), bf16[256,16,16]{0,2,1:T(8,128)(2,1)S(1)}, u32[]{:S(2)}, u32[]{:S(2)}) %all-to-all-start.3) | async-done | bytes 131104 | tf_op jit(solution)/shard_map/all_to_all | solution.py:90
  125.3 3.5 %all-to-all-start.5 = ((f32[16,256,16]{1,2,0:T(8,128)}), f32[16,256,16]{1,2,0:T(8,128)S(1)}, u32[]{:S(2)}, u32[]{:S(2)}) async-start(f32[16,256,16]{1,2,0:T(8,128)} %copy.279), calls=%async_computation.5 | async-start | bytes 524288 | tf_op jit(solution)/shard_map/all_to_all | solution.py:96
  129.2 3.3 fusion.66
  133.4 5.4 %all-to-all-done.5 = f32[16,256,16]{1,2,0:T(8,128)S(1)} async-done(((f32[16,256,16]{1,2,0:T(8,128)}), f32[16,256,16]{1,2,0:T(8,128)S(1)}, u32[]{:S(2)}, u32[]{:S(2)}) %all-to-all-start.5) | async-done | bytes 262176 | tf_op jit(solution)/shard_map/all_to_all | solution.py:96
  141.1 3.0 fusion.35
  144.1 2.9 fusion.37
  147.0 8.8 %all-gather.11.cloned.1.call-done = f32[1024,256]{0,1:T(8,128)} async-done(((f32[1024,16]{0,1:T(8,128)}), f32[1024,256]{0,1:T(8,128)}) %all-gather.11.cloned.1.call-update) | async-done | bytes 1048592 | tf_op jit(solution)/shard_map/all_gather | solution.py:105
  159.0 7.6 %fusion.1 = (f32[16,256,128]{1,2,0:T(8,128)}, f32[16,256,128]{1,2,0:T(8,128)}, f32[16,256,128]{1,2,0:T(8,128)}, f32[16,256,128]{1,2,0:T(8,128)}, f32[16,256,128]{1,2,0:T(8,128)}, /*index=5*/f32[16,256,128]{1,2,0:T(8,128)}) fusion(f32[128,16,256]{2,0,1:T(8,128)S(1)} %fusion.31, f32[16,128]{1,0:T(8,128)S(1)} %get-tuple-element.39, ...), kind=kOutput, calls=%fused_computation.3 | convolution fusion | flops 212451328 | bytes 24133632 | tf_op jit(solution)/shard_map/bca,ak->bck/dot_general | solution.py:10
  166.6 2.2 copy.290
  168.8 2.4 fusion.279
  171.3 3.1 copy.291
  174.3 4.1 %fusion.275 = f32[16,256,128]{2,0,1:T(8,128)} fusion(f32[16,256,128]{2,0,1:T(8,128)} %copy.291), kind=kOutput, calls=%fused_computation.340 | convolution fusion | flops 50335232 | bytes 4194304 | tf_op jit(solution)/shard_map/bck,bm->mck/dot_general | solution.py:10
  178.4 2.6 convolution_add_fusion.2
  181.0 3.1 copy.285
  184.1 4.0 %fusion.281 = f32[16,256,128]{2,0,1:T(8,128)} fusion(f32[16,256,128]{2,0,1:T(8,128)} %copy.285), kind=kOutput, calls=%fused_computation.346 | convolution fusion | flops 50335232 | bytes 4194304 | tf_op jit(solution)/shard_map/vmap(bck,bm->mck)/dot_general | solution.py:10
  188.0 3.4 copy.286
  191.5 2.8 fusion.277
  199.7 2.3 fusion.253
  202.0 2.4 fusion.271
  204.4 2.4 fusion.273
  206.9 2.4 fusion.251
  209.3 1.9 copy.296
  211.2 3.0 copy.297
  214.2 2.9 copy.298
  217.1 2.9 copy.299
  220.0 5.1 %fusion.14 = f32[16,256,128]{1,2,0:T(8,128)S(1)} fusion(f32[16,128]{1,0:T(8,128)S(1)} %get-tuple-element.39, f32[16,128]{1,0:T(8,128)S(1)} %get-tuple-element.40, f32[16,256,128]{1,2,0:T(8,128)} %copy.298, f32[16,256,128]{1,2,0:T(8,128)} %copy.299, f32[16,256,128]{1,2,0:T(8,128)S(1)} %copy.296, f32[16,256,128]{1,2,0:T(8,128)} %copy.297), kind=kOutput, calls=%fused_computation.32 | convolution fusion | flops 405504000 | bytes 10502144 | tf_op jit(solution)/shard_map/vmap(bck,ka->bca)/dot_general | solution.py:10
  225.2 1.9 multiply_bitcast_fusion.1
  231.9 3.5 %multiply_add_fusion.1 = (f32[16,256,128]{1,2,0:T(8,128)}, f32[16,256,128]{1,2,0:T(8,128)}) fusion(f32[16,256,128]{1,2,0:T(8,128)S(1)} %fusion.85, f32[16,128]{1,0:T(8,128)S(1)} %get-tuple-element.39, f32[16,128]{1,0:T(8,128)S(1)} %get-tuple-element.40, bf16[16,256,64]{1,0,2:T(8,128)(2,1)S(1)} %bitcast.381), kind=kOutput, calls=%fused_computation.30 | convolution fusion | flops 205111296 | bytes 6832128 | tf_op jit(solution)/shard_map/vmap(bca,ak->bck)/dot_general | solution.py:10
  235.5 2.2 copy.309
  237.7 2.4 fusion.269
  240.1 3.0 copy.311
  243.2 4.1 %fusion.265 = f32[16,256,128]{2,0,1:T(8,128)} fusion(f32[16,256,128]{2,0,1:T(8,128)} %copy.311), kind=kOutput, calls=%fused_computation.330 | convolution fusion | flops 50335232 | bytes 4194304 | tf_op jit(solution)/shard_map/vmap(bck,bm->mck)/dot_general | solution.py:10
  247.3 2.5 convolution_add_fusion.1
  249.8 3.0 copy.315
  252.9 4.0 %fusion.267 = f32[16,256,128]{2,0,1:T(8,128)} fusion(f32[16,256,128]{2,0,1:T(8,128)} %copy.315), kind=kOutput, calls=%fused_computation.332 | convolution fusion | flops 50335232 | bytes 4194304 | tf_op jit(solution)/shard_map/bck,bm->mck/dot_general | solution.py:10
  256.8 3.3 copy.316
  260.1 2.8 fusion.263
  266.8 2.9 multiply_subtract_fusion
  271.0 2.4 fusion.261
  273.4 3.1 copy.321
  276.5 2.4 fusion.245
  278.9 2.9 copy.322
  281.8 2.3 fusion.259
  284.1 3.1 copy.323
  287.2 2.3 fusion.243
  289.6 3.1 copy.324
  292.7 5.2 %fusion.6 = f32[16,256,128]{1,2,0:T(8,128)S(1)} fusion(f32[16,128]{1,0:T(8,128)S(1)} %get-tuple-element.39, f32[16,128]{1,0:T(8,128)S(1)} %get-tuple-element.40, f32[16,256,128]{1,2,0:T(8,128)} %copy.323, f32[16,256,128]{1,2,0:T(8,128)} %copy.324, f32[16,256,128]{1,2,0:T(8,128)S(1)} %copy-done.9, f32[16,256,128]{1,2,0:T(8,128)} %copy.322), kind=kOutput, calls=%fused_computation.19 | convolution fusion | flops 405504000 | bytes 10502144 | tf_op jit(solution)/shard_map/vmap(bck,ka->bca)/dot_general | solution.py:10
  297.9 1.9 multiply_bitcast_fusion
  304.5 28.4 %psum.7 = f32[1,1024]{1,0:T(1,128)S(1)} all-reduce(f32[1,1024]{1,0:T(1,128)S(1)} %bitcast.393), channel_id=1, replica_groups=mesh['ctx'=16,'ch'=16] {'ch'}, use_global_device_ids=true, to_apply=%region_1.2 | all-reduce | flops 1024 | bytes 8192 | tf_op jit(solution)/shard_map/psum | solution.py:146
  (189 shorter events, 72.2 us)
Async XLA Ops:
  7.2 19.1 %copy-start.39 = (bf16[256,256]{1,0:T(8,128)(2,1)S(1)}, bf16[256,256]{1,0:T(8,128)(2,1)}, u32[]{:S(2)}) copy-start(bf16[256,256]{1,0:T(8,128)(2,1)} %param.11) | copy-start | bytes 393220
  7.2 20.5 %copy-start.37 = (bf16[1,1024,256]{2,1,0:T(8,128)(2,1)S(1)}, bf16[1,1024,256]{2,1,0:T(8,128)(2,1)}, u32[]{:S(2)}) copy-start(bf16[1,1024,256]{2,1,0:T(8,128)(2,1)} %param.17) | copy-start | bytes 1572868
  7.2 21.5 %copy-start.40 = (bf16[256,256]{1,0:T(8,128)(2,1)S(1)}, bf16[256,256]{1,0:T(8,128)(2,1)}, u32[]{:S(2)}) copy-start(bf16[256,256]{1,0:T(8,128)(2,1)} %param.12) | copy-start | bytes 393220
  7.2 22.3 %copy-start.28 = (bf16[1,1024,256]{2,1,0:T(8,128)(2,1)S(1)}, bf16[1,1024,256]{2,1,0:T(8,128)(2,1)}, u32[]{:S(2)}) copy-start(bf16[1,1024,256]{2,1,0:T(8,128)(2,1)} %param.15) | copy-start | bytes 1572868
  9.0 21.4 %all-to-all-start.1 = ((bf16[256,16,16]{0,2,1:T(8,128)(2,1)}), bf16[256,16,16]{0,2,1:T(8,128)(2,1)S(1)}, u32[]{:S(2)}, u32[]{:S(2)}) async-start(bf16[256,16,16]{0,2,1:T(8,128)(2,1)} %bitcast.10), calls=%async_computation.1 | async-start | bytes 262144 | tf_op jit(solution)/shard_map/all_to_all | solution.py:91
  30.4 18.3 %all-to-all-start = ((bf16[256,16,16]{0,2,1:T(8,128)(2,1)}), bf16[256,16,16]{0,2,1:T(8,128)(2,1)S(1)}, u32[]{:S(2)}, u32[]{:S(2)}) async-start(bf16[256,16,16]{0,2,1:T(8,128)(2,1)} %bitcast.3), calls=%async_computation | async-start | bytes 262144 | tf_op jit(solution)/shard_map/all_to_all | solution.py:90
  39.4 100.1 %all-gather.9.cloned.1.call-start = ((), (), s32[]{:S(2)}) async-start(), calls=%async_computation.8 | async-start | bytes 1114112 | tf_op jit(solution)/shard_map/all_gather | solution.py:105
  48.7 12.7 %all-to-all-start.4 = ((bf16[256,16,16]{0,2,1:T(8,128)(2,1)}), bf16[256,16,16]{0,2,1:T(8,128)(2,1)S(1)}, u32[]{:S(2)}, u32[]{:S(2)}) async-start(bf16[256,16,16]{0,2,1:T(8,128)(2,1)} %bitcast.22), calls=%async_computation.4 | async-start | bytes 262144 | tf_op jit(solution)/shard_map/all_to_all | solution.py:91
  52.2 103.6 %all-gather.11.cloned.1.call-start = ((), (), s32[]{:S(2)}) async-start(), calls=%async_computation.9 | async-start | bytes 1114112 | tf_op jit(solution)/shard_map/all_gather | solution.py:105
  61.4 3.1 copy-start.34
  61.4 2.1 copy-start.25
  61.4 2.6 copy-start.26
  68.3 1.3 copy-start.27
  73.4 2.8 copy-start.35
  79.3 20.3 %all-to-all-start.2 = ((f32[16,256,16]{1,2,0:T(8,128)}), f32[16,256,16]{1,2,0:T(8,128)S(1)}, u32[]{:S(2)}, u32[]{:S(2)}) async-start(f32[16,256,16]{1,2,0:T(8,128)} %copy.269), calls=%async_computation.2 | async-start | bytes 524288 | tf_op jit(solution)/shard_map/all_to_all | solution.py:96
  82.9 145.9 %all-gather.7.cloned.1.call-start = ((), (), s32[]{:S(2)}) async-start(), calls=%async_computation.7 | async-start | bytes 1114112 | tf_op jit(solution)/shard_map/all_gather | solution.py:104
  84.7 0.7 copy-start.36
  101.3 12.9 %all-to-all-start.3 = ((bf16[256,16,16]{0,2,1:T(8,128)(2,1)}), bf16[256,16,16]{0,2,1:T(8,128)(2,1)S(1)}, u32[]{:S(2)}, u32[]{:S(2)}) async-start(bf16[256,16,16]{0,2,1:T(8,128)(2,1)} %bitcast.390), calls=%async_computation.3 | async-start | bytes 262144 | tf_op jit(solution)/shard_map/all_to_all | solution.py:90
  116.6 1.0 copy-start.32
  116.6 1.2 copy-start.33
  122.9 0.8 copy-start.31
  124.4 8.0 %slice-start = ((f32[256,32,16]{0,1,2:T(8,128)}), f32[32,32,16]{0,1,2:T(8,128)S(1)}, s32[]{:S(2)}) async-start(f32[256,32,16]{0,1,2:T(8,128)} %copy-done.31), calls=%async_computation.10 | async-start | bytes 524288 | tf_op jit(solution)/shard_map/slice | solution.py:101
  125.3 13.4 %all-to-all-start.5 = ((f32[16,256,16]{1,2,0:T(8,128)}), f32[16,256,16]{1,2,0:T(8,128)S(1)}, u32[]{:S(2)}, u32[]{:S(2)}) async-start(f32[16,256,16]{1,2,0:T(8,128)} %copy.279), calls=%async_computation.5 | async-start | bytes 524288 | tf_op jit(solution)/shard_map/all_to_all | solution.py:96
  128.8 9.9 %copy-start.38 = (bf16[256,256]{0,1:T(8,128)(2,1)S(1)}, bf16[256,256]{0,1:T(8,128)(2,1)}, u32[]{:S(2)}) copy-start(bf16[256,256]{0,1:T(8,128)(2,1)} %copy.260) | copy-start | bytes 393220
  128.9 172.6 %all-gather.5.cloned.1.call-start = ((), (), s32[]{:S(2)}) async-start(), calls=%async_computation.6 | async-start | bytes 1114112 | tf_op jit(solution)/shard_map/all_gather | solution.py:104
  157.4 1.6 copy-start.16
  174.3 4.1 %copy-start.5 = (f32[16,256,128]{2,0,1:T(8,128)S(1)}, f32[16,256,128]{2,0,1:T(8,128)}, u32[]{:S(2)}) copy-start(f32[16,256,128]{2,0,1:T(8,128)} %copy.291) | copy-start | bytes 6291460
  174.3 4.1 %copy-start.23 = (f32[16,256,128]{2,0,1:T(8,128)S(1)}, f32[16,256,128]{2,0,1:T(8,128)}, u32[]{:S(2)}) copy-start(f32[16,256,128]{2,0,1:T(8,128)} %fusion.279) | copy-start | bytes 6291460
  191.5 2.9 copy-start.6
  191.5 2.9 copy-start.24
  194.4 1.6 copy-start.20
  196.0 1.6 copy-start.2
  196.0 2.2 copy-start.18
  220.0 5.1 %copy-start.12 = (f32[16,256,128]{1,2,0:T(8,128)S(1)}, f32[16,256,128]{1,2,0:T(8,128)}, u32[]{:S(2)}) copy-start(f32[16,256,128]{1,2,0:T(8,128)} %copy.297) | copy-start | bytes 6291460
  220.0 5.2 %copy-start.14 = (f32[16,256,128]{1,2,0:T(8,128)S(1)}, f32[16,256,128]{1,2,0:T(8,128)}, u32[]{:S(2)}) copy-start(f32[16,256,128]{1,2,0:T(8,128)} %copy.298) | copy-start | bytes 6291460
  220.0 5.2 %copy-start.15 = (f32[16,256,128]{1,2,0:T(8,128)S(1)}, f32[16,256,128]{1,2,0:T(8,128)}, u32[]{:S(2)}) copy-start(f32[16,256,128]{1,2,0:T(8,128)} %copy.299) | copy-start | bytes 6291460
  228.3 1.1 copy-start.30
  243.1 4.1 %copy-start.7 = (f32[16,256,128]{2,0,1:T(8,128)S(1)}, f32[16,256,128]{2,0,1:T(8,128)}, u32[]{:S(2)}) copy-start(f32[16,256,128]{2,0,1:T(8,128)} %copy.311) | copy-start | bytes 6291460
  243.2 4.1 %copy-start.21 = (f32[16,256,128]{2,0,1:T(8,128)S(1)}, f32[16,256,128]{2,0,1:T(8,128)}, u32[]{:S(2)}) copy-start(f32[16,256,128]{2,0,1:T(8,128)} %fusion.269) | copy-start | bytes 6291460
  260.1 2.8 copy-start.8
  260.1 2.8 copy-start.22
  263.0 1.6 copy-start.4
  264.6 1.6 copy-start.17
  264.6 2.2 copy-start.19
  269.7 1.3 copy-start
  273.4 3.1 copy-start.3
  284.1 3.1 copy-start.1
  289.6 3.1 copy-start.9
  292.6 5.2 %copy-start.10 = (f32[16,256,128]{1,2,0:T(8,128)S(1)}, f32[16,256,128]{1,2,0:T(8,128)}, u32[]{:S(2)}) copy-start(f32[16,256,128]{1,2,0:T(8,128)} %copy.322) | copy-start | bytes 6291460
  292.6 5.2 %copy-start.11 = (f32[16,256,128]{1,2,0:T(8,128)S(1)}, f32[16,256,128]{1,2,0:T(8,128)}, u32[]{:S(2)}) copy-start(f32[16,256,128]{1,2,0:T(8,128)} %copy.323) | copy-start | bytes 6291460
  292.6 5.2 %copy-start.13 = (f32[16,256,128]{1,2,0:T(8,128)S(1)}, f32[16,256,128]{1,2,0:T(8,128)}, u32[]{:S(2)}) copy-start(f32[16,256,128]{1,2,0:T(8,128)} %copy.324) | copy-start | bytes 6291460
  301.0 1.0 copy-start.29
  301.0 1.0 copy-start.41
Sparse Core Ops, SparseCore 0:
  42.7 59.4 all-gather.8
  104.7 51.0 all-gather.10
  158.3 50.7 all-gather.6
  211.9 50.5 all-gather.4
where the time goes:
time: 348 us; the launch traced here: 342 us
  matrix products  132 us (38%)
  local copies, waits for them, and re-layouts  81.4 us (23%)
  waiting for transfers between devices  41.8 us (12%)
  starting transfers between devices  35.9 us (10%)
  blocking collectives  28.4 us (8%)
  between operations  17.5 us (5%)
  other arithmetic  5.46 us (2%)
    dot_general x72, matrix products, contract(): return jnp.einsum(form, left, right, precision=lax.Precision.HIGH)  132 us
    psum x1, blocking collectives, per_device(): projection = lax.psum(partial_value, 'ch')  28.4 us
    dot_general x8, local copies, waits for them, and re-layouts, contract(): return jnp.einsum(form, left, right, precision=lax.Precision.HIGH)  22.9 us
    unnamed x95, local copies, waits for them, and re-layouts  19.7 us
    all_to_all x2, starting transfers between devices, spread_channels(): lax.all_to_all(filter_taps, 'ctx', split_axis=1, concat_axis=0, tiled=True)  15.3 us
    all_to_all x2, waiting for transfers between devices, return_tokens(): lax.all_to_all(values, 'ctx', split_axis=0, concat_axis=1, tiled=True)  14.2 us
    sub x4, local copies, waits for them, and re-layouts, forward_spectrum(): twist_imag = part_imag * cos_twist - part_real * sin_twist  12.8 us
    all_to_all x2, starting transfers between devices, spread_channels(): lax.all_to_all(signal, 'ctx', split_axis=1, concat_axis=0, tiled=True)  12.7 us
  transfers between devices with their start and end apart: 10, of which 6 were waited for; matrix products, arithmetic and copies ran while one was open for 60% of the time, Pallas kernels for 0%

commit v1 on v0

v1 whole, which is shorter than its diff:
```python
import functools

import jax
import jax.numpy as jnp
import ml_dtypes
import numpy as np
from jax import lax
from jax.experimental import pallas as pl
from jax.experimental.pallas import tpu as pltpu
from jax.sharding import PartitionSpec as P

BLK = 256
NCTX = 16
NY = 4
NZ = NCTX // NY
OWN = BLK // NCTX
RBLK = 4
NOUT = NCTX + RBLK
MESH = pl.DeviceIdType.MESH
F32 = jnp.float32
BF16 = jnp.bfloat16


def dft_tables():
    k = np.arange(BLK, dtype=np.int64)[:, None]
    n = np.arange(BLK, dtype=np.int64)[None, :]
    angle = ((2 * k + 1) * n % (4 * BLK)).astype(np.float64) * (np.pi / (2 * BLK))
    table = np.concatenate([np.cos(angle), -np.sin(angle)], axis=0)
    high = table.astype(ml_dtypes.bfloat16)
    low = (table - high.astype(np.float64)).astype(ml_dtypes.bfloat16)
    return high, low, np.ascontiguousarray(high.T), np.ascontiguousarray(low.T)


def dot(a, b):
    return jnp.dot(a, b, preferred_element_type=F32)


def dot_nt(a, b):
    return lax.dot_general(a, b, (((1,), (1,)), ((), ())), preferred_element_type=F32)


def split(value):
    high = value.astype(BF16)
    low = (value - high.astype(F32)).astype(BF16)
    return high, low


def kernel(
    nch,
    x_ref,
    g1_ref,
    g2_ref,
    h1_ref,
    h2_ref,
    v_ref,
    ri_ref,
    ro_ref,
    len_ref,
    rd_ref,
    f_hi,
    f_lo,
    ft_hi,
    ft_lo,
    po_ref,
    out_ref,
    sc_ref,
    send_in,
    recv_in,
    xr_ref,
    xi_ref,
    hr_ref,
    hi_ref,
    q_ref,
    gath,
    back_send,
    back_recv,
    vs_ref,
    hs_ref,
    q_hi,
    q_lo,
    p_send,
    p_recv,
    in_send_sem,
    in_recv_sem,
    gz_send_sem,
    gz_recv_sem,
    gy_send_sem,
    gy_recv_sem,
    back_send_sem,
    back_recv_sem,
    p_send_sem,
    p_recv_sem,
):
    me = lax.axis_index("ctx")
    mc = lax.axis_index("ch")
    zh = me // NY
    yy = lax.rem(me, NY)

    def loop(low, high, body):
        def step(i, carry):
            body(i)
            return carry

        lax.fori_loop(low, high, step, 0)

    def ctx_peer(k):
        return lax.rem(me + k, NCTX)

    barrier = pltpu.get_barrier_semaphore()
    loop(
        1,
        NCTX,
        lambda k: pl.semaphore_signal(
            barrier, inc=1, device_id={"ctx": ctx_peer(k)}, device_id_type=MESH
        ),
    )
    if nch > 1:
        loop(
            1,
            nch,
            lambda k: pl.semaphore_signal(
                barrier, inc=1, device_id={"ch": lax.rem(mc + k, nch)}, device_id_type=MESH
            ),
        )

    mine = pl.ds(pl.multiple_of(me * OWN, OWN), OWN)
    stages = ((0, 2), (2, 2), (4, 1))

    def in_copy(stage, k):
        first, count = stages[stage]
        peer = ctx_peer(k)
        rows = pl.ds(pl.multiple_of(peer * OWN, OWN), OWN)
        return pltpu.make_async_remote_copy(
            src_ref=send_in.at[pl.ds(first, count), rows, :],
            dst_ref=recv_in.at[pl.ds(first, count), mine, :],
            send_sem=in_send_sem.at[stage, k],
            recv_sem=in_recv_sem.at[stage, k],
            device_id={"ctx": peer},
            device_id_type=MESH,
        )

    def pack(slot, ref):
        send_in[slot] = jnp.transpose(ref[...])
        recv_in[slot, mine, :] = send_in[slot, mine, :]

    pack(0, x_ref)
    pack(1, h1_ref)
    pl.semaphore_wait(barrier, NCTX - 1 + nch - 1)
    loop(1, NCTX, lambda k: in_copy(0, k).start())
    pack(2, g1_ref)
    pack(3, h2_ref)
    loop(1, NCTX, lambda k: in_copy(1, k).start())
    pack(4, g2_ref)
    loop(1, NCTX, lambda k: in_copy(2, k).start())

    rows_y = pl.ds(pl.multiple_of(yy * OWN, OWN), OWN)

    def gz_copy(kind, k):
        part = gath.at[kind, :, zh, rows_y, :]
        return pltpu.make_async_remote_copy(
            src_ref=part,
            dst_ref=part,
            send_sem=gz_send_sem.at[kind, k],
            recv_sem=gz_recv_sem.at[kind, k],
            device_id={"ctx": lax.rem(zh + k, NZ) * NY + yy},
            device_id_type=MESH,
        )

    def gy_copy(kind, k):
        part = gath.at[kind, :, :, rows_y, :]
        return pltpu.make_async_remote_copy(
            src_ref=part,
            dst_ref=part,
            send_sem=gy_send_sem.at[kind, k],
            recv_sem=gy_recv_sem.at[kind, k],
            device_id={"ctx": zh * NY + lax.rem(yy + k, NY)},
            device_id_type=MESH,
        )

    def share_z(kind, rows):
        for b in range(RBLK):
            gath[kind, b, zh, rows_y, :] = rows[b * OWN : (b + 1) * OWN]
        loop(1, NZ, lambda k: gz_copy(kind, k).start())

    def share_y(kind):
        loop(1, NZ, lambda k: gz_copy(kind, k).wait_recv())
        loop(1, NY, lambda k: gy_copy(kind, k).start())

    def shared(kind):
        loop(1, NY, lambda k: gy_copy(kind, k).wait_recv())

    def rows_spectrum(rows):
        return dot(rows, ft_hi[...]) + dot(rows, ft_lo[...])

    lane_sign = 1.0 - 2.0 * lax.rem(
        lax.broadcasted_iota(jnp.int32, (OWN, BLK), 1), 2
    ).astype(F32)

    def set_taps(rows):
        s = rows_spectrum(rows)
        for j in range(NCTX):
            hr_ref[j] = s[j * OWN : (j + 1) * OWN, :BLK]
            hi_ref[j] = s[j * OWN : (j + 1) * OWN, BLK:]

    def owner_convolution(rows):
        s = rows_spectrum(rows)
        prev = None
        for m in range(NCTX + 1):
            now = None
            if m < NCTX:
                now = (s[m * OWN : (m + 1) * OWN, :BLK], s[m * OWN : (m + 1) * OWN, BLK:])
            if prev is None:
                real, imag = now
            else:
                real, imag = -lane_sign * prev[1], lane_sign * prev[0]
                if now is not None:
                    real, imag = now[0] + real, now[1] + imag
            xr_ref[m] = real
            xi_ref[m] = imag
            prev = now
        for i in range(NOUT):
            real = imag = None
            for m in range(max(0, i - NCTX + 1), min(i, NCTX) + 1):
                xr, xi, hr, hi = xr_ref[m], xi_ref[m], hr_ref[i - m], hi_ref[i - m]
                pr = xr * hr - xi * hi
                pi = xr * hi + xi * hr
                real = pr if real is None else real + pr
                imag = pi if imag is None else imag + pi
            q_ref[i * OWN : (i + 1) * OWN, :BLK] = real
            q_ref[i * OWN : (i + 1) * OWN, BLK:] = imag
        high, low = split(q_ref[...])
        fh, fl = f_hi[...], f_lo[...]
        return (dot(high, fh) + dot(low, fh) + dot(high, fl)) * (1.0 / BLK)

    def columns_spectrum(store, block, nt):
        def one(b):
            a = block(b)
            mul = dot_nt if nt else dot
            store[b] = mul(f_hi[...], a) + mul(f_lo[...], a)

        loop(0, RBLK, one)

    chunk = 16
    row_sign = 1.0 - 2.0 * lax.rem(
        lax.broadcasted_iota(jnp.int32, (chunk, BLK), 0), 2
    ).astype(F32)

    def response_products():
        def one(n):
            at = pl.ds(pl.multiple_of(n * chunk, chunk), chunk)
            at_i = pl.ds(pl.multiple_of(BLK + n * chunk, chunk), chunk)
            sig = []
            prev = None
            for m in range(RBLK):
                now = (vs_ref[m, at, :], vs_ref[m, at_i, :])
                if prev is None:
                    sig.append(now)
                else:
                    sig.append((now[0] - row_sign * prev[1], now[1] + row_sign * prev[0]))
                prev = now
            tap = [(hs_ref[j, at, :], hs_ref[j, at_i, :]) for j in range(RBLK)]
            for i in range(RBLK):
                real = imag = None
                for m in range(i + 1):
                    (xr, xi), (hr, hi) = sig[m], tap[i - m]
                    pr = xr * hr - xi * hi
                    pi = xr * hi + xi * hr
                    real = pr if real is None else real + pr
                    imag = pi if imag is None else imag + pi
                q_hi[i, at, :], q_lo[i, at, :] = split(real * (1.0 / BLK))
                q_hi[i, at_i, :], q_lo[i, at_i, :] = split(imag * (1.0 / BLK))

        loop(0, BLK // chunk, one)

    def response_block(b):
        high, low = q_hi[b], q_lo[b]
        return dot(ft_hi[...], high) + dot(ft_hi[...], low) + dot(ft_lo[...], high)

    def tokens(b):
        return pl.ds(pl.multiple_of(b * BLK, BLK), BLK)

    def gathered(kind, b):
        return gath[kind, b].reshape(BLK, BLK)

    columns_spectrum(vs_ref, lambda b: v_ref[tokens(b), :], False)

    loop(1, NCTX, lambda k: in_copy(0, k).wait_recv())
    share_z(0, recv_in[1, : RBLK * OWN, :])
    set_taps(recv_in[1])
    conv = owner_convolution(recv_in[0])
    share_z(1, conv[BLK:].astype(BF16))
    share_y(0)
    loop(1, NCTX, lambda k: in_copy(1, k).wait_recv())
    share_z(2, recv_in[3, : RBLK * OWN, :])
    set_taps(recv_in[3])
    gated = (recv_in[2].astype(F32) * conv[:BLK]).astype(BF16)
    conv = owner_convolution(gated)
    share_z(3, conv[BLK:].astype(BF16))
    share_y(1)
    share_y(2)

    loop(1, NCTX, lambda k: in_copy(2, k).wait_recv())
    back_send[...] = (recv_in[4].astype(F32) * conv[:BLK]).astype(BF16)
    back_recv[mine, :] = back_send[mine, :]

    def back_copy(k):
        peer = ctx_peer(k)
        rows = pl.ds(pl.multiple_of(peer * OWN, OWN), OWN)
        return pltpu.make_async_remote_copy(
            src_ref=back_send.at[rows, :],
            dst_ref=back_recv.at[mine, :],
            send_sem=back_send_sem.at[k],
            recv_sem=back_recv_sem.at[k],
            device_id={"ctx": peer},
            device_id_type=MESH,
        )

    share_y(3)
    loop(1, NCTX, lambda k: back_copy(k).start())

    shared(0)
    columns_spectrum(hs_ref, lambda b: gathered(0, b), True)
    response_products()
    shared(1)

    def gate_one(b):
        total = jnp.transpose(gathered(1, b).astype(F32)) + response_block(b)
        gated_block = (ri_ref[tokens(b), :].astype(F32) * total).astype(BF16)
        vs_ref[b] = dot(f_hi[...], gated_block) + dot(f_lo[...], gated_block)

    loop(0, RBLK, gate_one)
    shared(2)
    columns_spectrum(hs_ref, lambda b: gathered(2, b), True)
    response_products()
    shared(3)

    length = len_ref[0]
    weight = jnp.broadcast_to(rd_ref[...], (16, BLK))
    w_hi = weight.astype(BF16).astype(F32)
    w_mid = (weight - w_hi).astype(BF16).astype(F32)
    w_lo = weight - w_hi - w_mid
    w_row = lax.broadcasted_iota(jnp.int32, (16, BLK), 0)
    weight = jnp.where(
        w_row == 0, w_hi, jnp.where(w_row == 1, w_mid, jnp.where(w_row == 2, w_lo, 0.0))
    ).astype(BF16)

    for b in range(RBLK):
        rows = pl.ds(b * BLK, BLK)
        total = jnp.transpose(gathered(3, b).astype(F32)) + response_block(b)
        value = ro_ref[rows, :].astype(F32) * total
        token = lax.broadcasted_iota(jnp.int32, (BLK, BLK), 0) + b * BLK
        block = jnp.where(token < length, value, 0.0).astype(BF16)
        out_ref[rows, :] = block
        part = jnp.sum(dot_nt(weight, block), axis=0, keepdims=True)
        p_send[2 * b : 2 * b + 1, :] = part[:, :128]
        p_send[2 * b + 1 : 2 * b + 2, :] = part[:, 128:]

    def p_copy(k):
        return pltpu.make_async_remote_copy(
            src_ref=p_send,
            dst_ref=p_recv.at[mc],
            send_sem=p_send_sem.at[k],
            recv_sem=p_recv_sem.at[k],
            device_id={"ch": lax.rem(mc + k, nch)},
            device_id_type=MESH,
        )

    p_recv[mc] = p_send[...]
    if nch > 1:
        loop(1, nch, lambda k: p_copy(k).start())

    loop(1, NCTX, lambda k: back_copy(k).wait_recv())
    po_ref[...] = jnp.transpose(back_recv[...])

    if nch > 1:
        loop(1, nch, lambda k: p_copy(k).wait_recv())
    projection = p_recv[0]
    for c in range(1, nch):
        projection = projection + p_recv[c]
    token = (
        lax.broadcasted_iota(jnp.int32, (8, 128), 0) * 128
        + lax.broadcasted_iota(jnp.int32, (8, 128), 1)
    )
    squares = jnp.where(token < length, projection * projection, 0.0)
    sc_ref[0] = jnp.sum(squares) / length.astype(F32)

    for stage in range(len(stages)):
        loop(1, NCTX, lambda k: in_copy(stage, k).wait_send())
    for kind in range(4):
        loop(1, NZ, lambda k: gz_copy(kind, k).wait_send())
        loop(1, NY, lambda k: gy_copy(kind, k).wait_send())
    loop(1, NCTX, lambda k: back_copy(k).wait_send())
    if nch > 1:
        loop(1, nch, lambda k: p_copy(k).wait_send())


def per_device(
    nch,
    prefix_values,
    inner_gate,
    outer_gate,
    inner_filter,
    outer_filter,
    response_values,
    response_inner,
    response_outer,
    lengths,
    readout,
):
    vmem = pl.BlockSpec(memory_space=pltpu.VMEM)
    smem = pl.BlockSpec(memory_space=pltpu.SMEM)
    dma = pltpu.SemaphoreType.DMA
    tokens = RBLK * BLK
    prefix_output, response_output, scores = pl.pallas_call(
        functools.partial(kernel, nch),
        out_shape=(
            jax.ShapeDtypeStruct((BLK, BLK), BF16),
            jax.ShapeDtypeStruct((tokens, BLK), BF16),
            jax.ShapeDtypeStruct((1,), F32),
        ),
        in_specs=[vmem] * 8 + [smem] + [vmem] * 5,
        out_specs=(vmem, vmem, smem),
        scratch_shapes=[
            pltpu.VMEM((5, BLK, BLK), BF16),
            pltpu.VMEM((5, BLK, BLK), BF16),
            pltpu.VMEM((NCTX + 1, OWN, BLK), F32),
            pltpu.VMEM((NCTX + 1, OWN, BLK), F32),
            pltpu.VMEM((NCTX, OWN, BLK), F32),
            pltpu.VMEM((NCTX, OWN, BLK), F32),
            pltpu.VMEM((NOUT * OWN, 2 * BLK), F32),
            pltpu.VMEM((4, RBLK, NZ, NY * OWN, BLK), BF16),
            pltpu.VMEM((BLK, BLK), BF16),
            pltpu.VMEM((BLK, BLK), BF16),
            pltpu.VMEM((RBLK, 2 * BLK, BLK), F32),
            pltpu.VMEM((RBLK, 2 * BLK, BLK), F32),
            pltpu.VMEM((RBLK, 2 * BLK, BLK), BF16),
            pltpu.VMEM((RBLK, 2 * BLK, BLK), BF16),
            pltpu.VMEM((8, 128), F32),
            pltpu.VMEM((nch, 8, 128), F32),
            dma((3, NCTX)),
            dma((3, NCTX)),
            dma((4, NZ)),
            dma((4, NZ)),
            dma((4, NY)),
            dma((4, NY)),
            dma((NCTX,)),
            dma((NCTX,)),
            dma((nch,)),
            dma((nch,)),
        ],
        compiler_params=pltpu.CompilerParams(
            collective_id=0, has_side_effects=True, vmem_limit_bytes=48 * 1024 * 1024
        ),
        cost_estimate=pl.CostEstimate(
            flops=8_000_000_000, bytes_accessed=5_000_000, transcendentals=0
        ),
        name="gated_convolutions",
    )(
        prefix_values,
        inner_gate,
        outer_gate,
        inner_filter,
        outer_filter,
        response_values.reshape(tokens, BLK),
        response_inner.reshape(tokens, BLK),
        response_outer.reshape(tokens, BLK),
        lengths,
        readout.reshape(1, BLK),
        *[jnp.asarray(t) for t in dft_tables()],
    )
    return prefix_output, response_output.reshape(1, tokens, BLK), scores


def solution(mesh):
    in_specs = (
        P("ctx", "ch"),
        P("ctx", "ch"),
        P("ctx", "ch"),
        P("ctx", "ch"),
        P("ctx", "ch"),
        P("ctx", None, "ch"),
        P("ctx", None, "ch"),
        P("ctx", None, "ch"),
        P("ctx"),
        P("ch"),
    )
    out_specs = (P("ctx", "ch"), P("ctx", None, "ch"), P("ctx"))
    return jax.shard_map(
        functools.partial(per_device, mesh.shape["ch"]),
        mesh=mesh,
        in_specs=in_specs,
        out_specs=out_specs,
        check_vma=False,
    )
```

time: 348 us -> 83.6 us (0.24); the launches traced: 342 us -> 83.1 us
  matrix products: 132 us -> 0 us
  local copies, waits for them, and re-layouts: 81.4 us -> 13.6 us
  Pallas kernels: 0 us -> 66.5 us
  waiting for transfers between devices: 41.8 us -> 0 us
  starting transfers between devices: 35.9 us -> 0 us
  blocking collectives: 28.4 us -> 0 us
  between operations: 17.5 us -> 3 us
  other arithmetic: 5.46 us -> 0 us
    dot_general x72 -> x0, matrix products: 132 us -> none  [contract(): return jnp.einsum(form, left, right, precision=lax.Precision.HIGH)]
    pallas_call x0 -> x1, Pallas kernels: none -> 66.5 us  [per_device(): pl.pallas_call(functools.partial(kernel, nch), out_shape=(jax.ShapeDtypeS...]
    all_to_all x6 -> x0, starting transfers between devices: 35 us -> none  [the longest x2 15.3 us: spread_channels(): lax.all_to_all(filter_taps, 'ctx', split_axis=1, concat_axis=0, tiled=True)]
    all_to_all x6 -> x0, waiting for transfers between devices: 32.9 us -> none  [the longest x2 14.2 us: return_tokens(): lax.all_to_all(values, 'ctx', split_axis=0, concat_axis=1, tiled=True)]
    psum x1 -> x0, blocking collectives: 28.4 us -> none  [per_device(): projection = lax.psum(partial_value, 'ch')]
    dot_general x8 -> x0, local copies, waits for them, and re-layouts: 22.9 us -> none  [contract(): return jnp.einsum(form, left, right, precision=lax.Precision.HIGH)]
    sub x4 -> x0, local copies, waits for them, and re-layouts: 12.8 us -> none  [forward_spectrum(): twist_imag = part_imag * cos_twist - part_real * sin_twist]
    add x4 -> x0, local copies, waits for them, and re-layouts: 10.6 us -> none  [forward_spectrum(): twist_real = part_real * cos_twist + part_imag * sin_twist]
  transfers between devices with their start and end apart: 10 -> 0, of which waited for: 6 -> 0; matrix products, arithmetic and copies ran while one was open for 60% -> 0% of each run, Pallas kernels for 0% -> 0%
where the time goes in v1:
time: 83.6 us; the launch traced here: 83.1 us
  Pallas kernels  66.5 us (80%)
  local copies, waits for them, and re-layouts  13.6 us (16%)
  between operations  3 us (4%)
    pallas_call x1, Pallas kernels, per_device(): pl.pallas_call(functools.partial(kernel, nch), out_shape=(jax.ShapeDtypeS...  66.5 us
    unnamed x28, local copies, waits for them, and re-layouts  13.6 us

profile of v1, /device:TPU:1, one launch (start us, length us, event | category | flops | bytes accessed | tf_op | source)
XLA Modules:
  0.0 83.1 jit_solution(9672072209685698993)
XLA Ops:
  1.3 0.0 copy-start.8
  1.3 0.7 copy-done.8
  2.0 0.0 copy-start
  2.0 1.0 %copy-done = bf16[1,1024,256]{2,1,0:T(8,128)(2,1)S(1)} copy-done((bf16[1,1024,256]{2,1,0:T(8,128)(2,1)S(1)}, bf16[1,1024,256]{2,1,0:T(8,128)(2,1)}, u32[]{:S(2)}) %copy-start) | copy-done | bytes 524312
  3.0 0.0 copy-start.1
  3.0 1.0 %copy-done.1 = bf16[1,1024,256]{2,1,0:T(8,128)(2,1)S(1)} copy-done((bf16[1,1024,256]{2,1,0:T(8,128)(2,1)S(1)}, bf16[1,1024,256]{2,1,0:T(8,128)(2,1)}, u32[]{:S(2)}) %copy-start.1) | copy-done | bytes 524312
  4.0 0.0 copy-start.2
  4.0 1.0 %copy-done.2 = bf16[1,1024,256]{2,1,0:T(8,128)(2,1)S(1)} copy-done((bf16[1,1024,256]{2,1,0:T(8,128)(2,1)S(1)}, bf16[1,1024,256]{2,1,0:T(8,128)(2,1)}, u32[]{:S(2)}) %copy-start.2) | copy-done | bytes 524312
  5.1 0.0 copy-start.3
  5.1 0.9 %copy-done.3 = bf16[256,256]{1,0:T(8,128)(2,1)S(1)} copy-done((bf16[256,256]{1,0:T(8,128)(2,1)S(1)}, bf16[256,256]{1,0:T(8,128)(2,1)}, u32[]{:S(2)}) %copy-start.3) | copy-done | bytes 131096
  6.0 0.0 copy-start.4
  6.0 0.9 %copy-done.4 = bf16[256,256]{1,0:T(8,128)(2,1)S(1)} copy-done((bf16[256,256]{1,0:T(8,128)(2,1)S(1)}, bf16[256,256]{1,0:T(8,128)(2,1)}, u32[]{:S(2)}) %copy-start.4) | copy-done | bytes 131096
  6.9 0.0 copy-start.5
  6.9 0.9 %copy-done.5 = bf16[256,256]{1,0:T(8,128)(2,1)S(1)} copy-done((bf16[256,256]{1,0:T(8,128)(2,1)S(1)}, bf16[256,256]{1,0:T(8,128)(2,1)}, u32[]{:S(2)}) %copy-start.5) | copy-done | bytes 131096
  7.8 0.0 copy-start.6
  7.8 0.9 %copy-done.6 = bf16[256,256]{1,0:T(8,128)(2,1)S(1)} copy-done((bf16[256,256]{1,0:T(8,128)(2,1)S(1)}, bf16[256,256]{1,0:T(8,128)(2,1)}, u32[]{:S(2)}) %copy-start.6) | copy-done | bytes 131096
  8.7 0.0 copy-start.7
  8.7 0.9 %copy-done.7 = bf16[256,256]{1,0:T(8,128)(2,1)S(1)} copy-done((bf16[256,256]{1,0:T(8,128)(2,1)S(1)}, bf16[256,256]{1,0:T(8,128)(2,1)}, u32[]{:S(2)}) %copy-start.7) | copy-done | bytes 131096
  9.6 0.0 copy-start.9
  9.6 0.9 %copy-done.9 = bf16[256,512]{1,0:T(8,128)(2,1)S(1)} copy-done((bf16[256,512]{1,0:T(8,128)(2,1)S(1)}, bf16[256,512]{1,0:T(8,128)(2,1)}, u32[]{:S(2)}) %copy-start.9) | copy-done | bytes 262168
  10.6 0.0 copy-start.10
  10.6 0.9 %copy-done.10 = bf16[256,512]{1,0:T(8,128)(2,1)S(1)} copy-done((bf16[256,512]{1,0:T(8,128)(2,1)S(1)}, bf16[256,512]{1,0:T(8,128)(2,1)}, u32[]{:S(2)}) %copy-start.10) | copy-done | bytes 262168
  11.5 0.0 copy-start.11
  11.5 0.9 %copy-done.11 = bf16[512,256]{1,0:T(8,128)(2,1)S(1)} copy-done((bf16[512,256]{1,0:T(8,128)(2,1)S(1)}, bf16[512,256]{1,0:T(8,128)(2,1)}, u32[]{:S(2)}) %copy-start.11) | copy-done | bytes 262168
  12.5 0.0 copy-start.12
  12.5 0.9 %copy-done.12 = bf16[512,256]{1,0:T(8,128)(2,1)S(1)} copy-done((bf16[512,256]{1,0:T(8,128)(2,1)S(1)}, bf16[512,256]{1,0:T(8,128)(2,1)}, u32[]{:S(2)}) %copy-start.12) | copy-done | bytes 262168
  13.4 66.5 %gated_convolutions.1 = (bf16[256,256]{1,0:T(8,128)(2,1)S(1)}, bf16[1024,256]{1,0:T(8,128)(2,1)S(1)}, f32[1]{0:T(128)}) custom-call(bf16[256,256]{1,0:T(8,128)(2,1)S(1)} %copy-done.3, bf16[256,256]{1,0:T(8,128)(2,1)S(1)} %copy-done.4, bf16[256,256]{1,0:T(8,128)(2,1)S(1)} %copy-done.5, bf16[256,256]{1,0:T(8,128)(2,1)S(1)} %copy-done.6, ...), custom_call_target="tpu_custom_call" | custom-call | flops 8000000000 | bytes 5000000 | tf_op jit(solution)/shard_map/gated_convolutions/pallas_call | solution.py:414
  79.9 0.7 copy.21
  80.6 0.8 copy.22
Async XLA Ops:
  1.3 0.7 copy-start.8
  2.0 1.0 %copy-start = (bf16[1,1024,256]{2,1,0:T(8,128)(2,1)S(1)}, bf16[1,1024,256]{2,1,0:T(8,128)(2,1)}, u32[]{:S(2)}) copy-start(bf16[1,1024,256]{2,1,0:T(8,128)(2,1)} %param.19) | copy-start | bytes 1572868
  3.0 1.0 %copy-start.1 = (bf16[1,1024,256]{2,1,0:T(8,128)(2,1)S(1)}, bf16[1,1024,256]{2,1,0:T(8,128)(2,1)}, u32[]{:S(2)}) copy-start(bf16[1,1024,256]{2,1,0:T(8,128)(2,1)} %param.20) | copy-start | bytes 1572868
  4.0 1.0 %copy-start.2 = (bf16[1,1024,256]{2,1,0:T(8,128)(2,1)S(1)}, bf16[1,1024,256]{2,1,0:T(8,128)(2,1)}, u32[]{:S(2)}) copy-start(bf16[1,1024,256]{2,1,0:T(8,128)(2,1)} %param.21) | copy-start | bytes 1572868
  5.1 0.9 %copy-start.3 = (bf16[256,256]{1,0:T(8,128)(2,1)S(1)}, bf16[256,256]{1,0:T(8,128)(2,1)}, u32[]{:S(2)}) copy-start(bf16[256,256]{1,0:T(8,128)(2,1)} %x_ref.1) | copy-start | bytes 393220
  6.0 0.9 %copy-start.4 = (bf16[256,256]{1,0:T(8,128)(2,1)S(1)}, bf16[256,256]{1,0:T(8,128)(2,1)}, u32[]{:S(2)}) copy-start(bf16[256,256]{1,0:T(8,128)(2,1)} %g1_ref.1) | copy-start | bytes 393220
  6.9 0.9 %copy-start.5 = (bf16[256,256]{1,0:T(8,128)(2,1)S(1)}, bf16[256,256]{1,0:T(8,128)(2,1)}, u32[]{:S(2)}) copy-start(bf16[256,256]{1,0:T(8,128)(2,1)} %g2_ref.1) | copy-start | bytes 393220
  7.8 0.9 %copy-start.6 = (bf16[256,256]{1,0:T(8,128)(2,1)S(1)}, bf16[256,256]{1,0:T(8,128)(2,1)}, u32[]{:S(2)}) copy-start(bf16[256,256]{1,0:T(8,128)(2,1)} %h1_ref.1) | copy-start | bytes 393220
  8.7 0.9 %copy-start.7 = (bf16[256,256]{1,0:T(8,128)(2,1)S(1)}, bf16[256,256]{1,0:T(8,128)(2,1)}, u32[]{:S(2)}) copy-start(bf16[256,256]{1,0:T(8,128)(2,1)} %h2_ref.1) | copy-start | bytes 393220
  9.6 0.9 %copy-start.9 = (bf16[256,512]{1,0:T(8,128)(2,1)S(1)}, bf16[256,512]{1,0:T(8,128)(2,1)}, u32[]{:S(2)}) copy-start(bf16[256,512]{1,0:T(8,128)(2,1)} %constant.11.clone.ft_lo) | copy-start | bytes 786436
  10.6 0.9 %copy-start.10 = (bf16[256,512]{1,0:T(8,128)(2,1)S(1)}, bf16[256,512]{1,0:T(8,128)(2,1)}, u32[]{:S(2)}) copy-start(bf16[256,512]{1,0:T(8,128)(2,1)} %constant.10.clone.ft_hi) | copy-start | bytes 786436
  11.5 0.9 %copy-start.11 = (bf16[512,256]{1,0:T(8,128)(2,1)S(1)}, bf16[512,256]{1,0:T(8,128)(2,1)}, u32[]{:S(2)}) copy-start(bf16[512,256]{1,0:T(8,128)(2,1)} %constant.9.clone.f_lo) | copy-start | bytes 786436
  12.5 0.9 %copy-start.12 = (bf16[512,256]{1,0:T(8,128)(2,1)S(1)}, bf16[512,256]{1,0:T(8,128)(2,1)}, u32[]{:S(2)}) copy-start(bf16[512,256]{1,0:T(8,128)(2,1)} %constant.8.clone.f_hi) | copy-start | bytes 786436

commit v2 on v1

v2 whole, which is shorter than its diff:
```python
import functools

import jax
import jax.numpy as jnp
import ml_dtypes
import numpy as np
from jax import lax
from jax.experimental import pallas as pl
from jax.experimental.pallas import tpu as pltpu
from jax.sharding import PartitionSpec as P

BLK = 256
NCTX = 16
NY = 4
NZ = NCTX // NY
OWN = BLK // NCTX
RBLK = 4
WORK = BLK // NY
NOUT = NCTX + RBLK
MESH = pl.DeviceIdType.MESH
F32 = jnp.float32
BF16 = jnp.bfloat16


def dft_tables():
    k = np.arange(BLK, dtype=np.int64)[:, None]
    n = np.arange(BLK, dtype=np.int64)[None, :]
    angle = ((2 * k + 1) * n % (4 * BLK)).astype(np.float64) * (np.pi / (2 * BLK))
    table = np.concatenate([np.cos(angle), -np.sin(angle)], axis=0)
    high = table.astype(ml_dtypes.bfloat16)
    low = (table - high.astype(np.float64)).astype(ml_dtypes.bfloat16)
    return high, low, np.ascontiguousarray(high.T), np.ascontiguousarray(low.T)


def dot(a, b):
    return jnp.dot(a, b, preferred_element_type=F32)


def split(value):
    high = value.astype(BF16)
    low = (value - high.astype(F32)).astype(BF16)
    return high, low


def kernel(
    nch,
    x_hbm,
    g1_hbm,
    g2_hbm,
    h1_hbm,
    h2_hbm,
    v_hbm,
    ri_hbm,
    ro_hbm,
    len_ref,
    rd_hbm,
    f_hi_hbm,
    f_lo_hbm,
    ft_hi_hbm,
    ft_lo_hbm,
    po_hbm,
    out_hbm,
    sc_ref,
    po_ref,
    out_ref,
    store_sem,
    x_ref,
    g1_ref,
    g2_ref,
    h1_ref,
    h2_ref,
    v_ref,
    ri_ref,
    ro_ref,
    rd_ref,
    f_hi,
    f_lo,
    ft_hi,
    ft_lo,
    load_sem,
    send_in,
    recv_in,
    resp_send,
    resp_recv,
    xr_ref,
    xi_ref,
    hr_ref,
    hi_ref,
    q_ref,
    gath,
    back_send,
    back_recv,
    vs_ref,
    hs_ref,
    q_hi,
    q_lo,
    out_send,
    out_home,
    p_send,
    p_recv,
    in_send_sem,
    in_recv_sem,
    resp_send_sem,
    resp_recv_sem,
    gz_send_sem,
    gz_recv_sem,
    last_send_sem,
    last_recv_sem,
    back_send_sem,
    back_recv_sem,
    out_send_sem,
    out_recv_sem,
    p_send_sem,
    p_recv_sem,
):
    me = lax.axis_index("ctx")
    mc = lax.axis_index("ch")
    zh = me // NY
    yy = lax.rem(me, NY)

    def loop(low, high, body):
        def step(i, carry):
            body(i)
            return carry

        lax.fori_loop(low, high, step, 0)

    def rows_of(index, size):
        return pl.ds(pl.multiple_of(index * size, size), size)

    def ctx_peer(k):
        return lax.rem(me + k, NCTX)

    def y_peer(k):
        return lax.rem(yy + k, NY)

    def group_of(index):
        return lax.rem(index, NY) * NZ + index // NY

    loads = {}
    for index, (source, target) in enumerate(
        (
            (x_hbm, x_ref),
            (h1_hbm, h1_ref),
            (g1_hbm, g1_ref),
            (h2_hbm, h2_ref),
            (v_hbm, v_ref),
            (ri_hbm, ri_ref),
            (ro_hbm, ro_ref),
            (ft_hi_hbm, ft_hi),
            (ft_lo_hbm, ft_lo),
            (f_hi_hbm, f_hi),
            (f_lo_hbm, f_lo),
            (g2_hbm, g2_ref),
            (rd_hbm, rd_ref),
        )
    ):
        loads[id(target)] = pltpu.make_async_copy(source, target, load_sem.at[index])
        loads[id(target)].start()

    def loaded(*refs):
        for ref in refs:
            loads[id(ref)].wait()

    barrier = pltpu.get_barrier_semaphore()
    loop(
        1,
        NCTX,
        lambda k: pl.semaphore_signal(
            barrier, inc=1, device_id={"ctx": ctx_peer(k)}, device_id_type=MESH
        ),
    )
    if nch > 1:
        loop(
            1,
            nch,
            lambda k: pl.semaphore_signal(
                barrier, inc=1, device_id={"ch": lax.rem(mc + k, nch)}, device_id_type=MESH
            ),
        )

    mine = rows_of(me, OWN)
    my_group = rows_of(group_of(me), OWN)

    def in_copy(stage, k):
        peer = ctx_peer(k)
        return pltpu.make_async_remote_copy(
            src_ref=send_in.at[pl.ds(2 * stage, 2), rows_of(group_of(peer), OWN), :],
            dst_ref=recv_in.at[pl.ds(2 * stage, 2), mine, :],
            send_sem=in_send_sem.at[stage, k],
            recv_sem=in_recv_sem.at[stage, k],
            device_id={"ctx": peer},
            device_id_type=MESH,
        )

    def pack(slot, ref):
        loaded(ref)
        send_in[slot] = jnp.transpose(ref[...])
        recv_in[slot, mine, :] = send_in[slot, my_group, :]

    def resp_copy(which, k):
        peer = y_peer(k)
        return pltpu.make_async_remote_copy(
            src_ref=resp_send.at[which, rows_of(peer, WORK), :],
            dst_ref=resp_recv.at[which, yy],
            send_sem=resp_send_sem.at[which, k],
            recv_sem=resp_recv_sem.at[which, k],
            device_id={"ctx": zh * NY + peer},
            device_id_type=MESH,
        )

    def turn(which, ref):
        loaded(ref)
        for b in range(RBLK):
            at = slice(b * BLK, (b + 1) * BLK)
            resp_send[which, :, at] = jnp.transpose(ref[at, :])

    def send_response(which, ref):
        turn(which, ref)
        loop(1, NY, lambda k: resp_copy(which, k).start())
        resp_recv[which, yy] = resp_send[which, rows_of(yy, WORK), :]

    def have_response(which):
        loop(1, NY, lambda k: resp_copy(which, k).wait_recv())

    def response(which, b):
        return resp_recv[which, :, :, b * BLK : (b + 1) * BLK].reshape(BLK, BLK)

    def z_index(step):
        return lax.rem(zh + step, NZ)

    def gz_copy(kind, k):
        part = gath.at[kind, :, zh]
        return pltpu.make_async_remote_copy(
            src_ref=part,
            dst_ref=part,
            send_sem=gz_send_sem.at[kind, k],
            recv_sem=gz_recv_sem.at[kind, k],
            device_id={"ctx": z_index(k) * NY + yy},
            device_id_type=MESH,
        )

    def last_copy(b, k):
        part = gath.at[3, b, zh]
        return pltpu.make_async_remote_copy(
            src_ref=part,
            dst_ref=part,
            send_sem=last_send_sem.at[b, k],
            recv_sem=last_recv_sem.at[b, k],
            device_id={"ctx": z_index(k) * NY + yy},
            device_id_type=MESH,
        )

    def store_rows(kind, rows):
        for b in range(RBLK):
            gath[kind, b, zh] = rows[b * OWN : (b + 1) * OWN]

    def share(kind, rows):
        store_rows(kind, rows)
        loop(1, NZ, lambda k: gz_copy(kind, k).start())

    def shared(kind):
        loop(1, NZ, lambda k: gz_copy(kind, k).wait_recv())

    def share_last(rows):
        store_rows(3, rows)
        for b in range(RBLK):
            loop(1, NZ, lambda k: last_copy(b, k).start())

    def tail(kind, b):
        rows = gath[kind, b].astype(F32).reshape(WORK, BLK)
        return jnp.concatenate([rows] * NY, axis=0)

    def spectrum(rows):
        return dot(rows, ft_hi[...]) + dot(rows, ft_lo[...])

    def inverse(high, low):
        return dot(high, f_hi[...]) + dot(low, f_hi[...]) + dot(high, f_lo[...])

    sign = 1.0 - 2.0 * lax.rem(lax.broadcasted_iota(jnp.int32, (OWN, BLK), 1), 2).astype(F32)

    def set_taps(rows):
        s = spectrum(rows)
        for j in range(NCTX):
            hr_ref[j] = s[j * OWN : (j + 1) * OWN, :BLK]
            hi_ref[j] = s[j * OWN : (j + 1) * OWN, BLK:]

    def owner_convolution(rows):
        s = spectrum(rows)
        prev = None
        for m in range(NCTX + 1):
            now = None
            if m < NCTX:
                now = (s[m * OWN : (m + 1) * OWN, :BLK], s[m * OWN : (m + 1) * OWN, BLK:])
            if prev is None:
                real, imag = now
            else:
                real, imag = -sign * prev[1], sign * prev[0]
                if now is not None:
                    real, imag = now[0] + real, now[1] + imag
            xr_ref[m] = real
            xi_ref[m] = imag
            prev = now
        for i in range(NOUT):
            real = imag = None
            for m in range(max(0, i - NCTX + 1), min(i, NCTX) + 1):
                xr, xi, hr, hi = xr_ref[m], xi_ref[m], hr_ref[i - m], hi_ref[i - m]
                pr = xr * hr - xi * hi
                pi = xr * hi + xi * hr
                real = pr if real is None else real + pr
                imag = pi if imag is None else imag + pi
            q_ref[i * OWN : (i + 1) * OWN, :BLK] = real
            q_ref[i * OWN : (i + 1) * OWN, BLK:] = imag
        return inverse(*split(q_ref[...])) * (1.0 / BLK)

    def head_spectrum(kind):
        hs_ref[...] = spectrum(gath[kind].reshape(RBLK * WORK, BLK))

    def response_products(blocks):
        def one(n):
            at = rows_of(n, OWN)
            tap_row = lax.rem(n, NZ) * OWN
            sig = []
            prev = None
            for m in range(blocks[-1] + 1):
                now = (vs_ref[m, at, :BLK], vs_ref[m, at, BLK:])
                if prev is None:
                    sig.append(now)
                else:
                    sig.append((now[0] - sign * prev[1], now[1] + sign * prev[0]))
                prev = now
            tap = []
            for j in range(blocks[-1] + 1):
                rows = pl.ds(pl.multiple_of(j * WORK + tap_row, OWN), OWN)
                tap.append((hs_ref[rows, :BLK], hs_ref[rows, BLK:]))
            for i in blocks:
                real = imag = None
                for m in range(i + 1):
                    (xr, xi), (hr, hi) = sig[m], tap[i - m]
                    pr = xr * hr - xi * hi
                    pi = xr * hi + xi * hr
                    real = pr if real is None else real + pr
                    imag = pi if imag is None else imag + pi
                q_hi[i, at, :BLK], q_lo[i, at, :BLK] = split(real * (1.0 / BLK))
                q_hi[i, at, BLK:], q_lo[i, at, BLK:] = split(imag * (1.0 / BLK))

        loop(0, BLK // OWN, one)

    pack(0, x_ref)
    pack(1, h1_ref)
    pl.semaphore_wait(barrier, NCTX - 1 + nch - 1)
    loop(1, NCTX, lambda k: in_copy(0, k).start())
    pack(2, g1_ref)
    pack(3, h2_ref)
    loop(1, NCTX, lambda k: in_copy(1, k).start())
    send_response(0, v_ref)
    send_response(1, ri_ref)
    turn(2, ro_ref)
    loaded(ft_hi, ft_lo, f_hi, f_lo, g2_ref, rd_ref)

    loop(1, NCTX, lambda k: in_copy(0, k).wait_recv())
    share(0, recv_in[1, : RBLK * OWN, :])
    set_taps(recv_in[1])
    conv = owner_convolution(recv_in[0])
    share(1, conv[BLK:].astype(BF16))

    have_response(0)
    for b in range(RBLK):
        vs_ref[b] = spectrum(response(0, b))

    loop(1, NCTX, lambda k: in_copy(1, k).wait_recv())
    share(2, recv_in[3, : RBLK * OWN, :])
    set_taps(recv_in[3])
    gated = (recv_in[2].astype(F32) * conv[:BLK]).astype(BF16)
    conv = owner_convolution(gated)
    share_last(conv[BLK:].astype(BF16))
    back_send[...] = conv[:BLK].astype(BF16)

    shared(0)
    head_spectrum(0)
    response_products(range(RBLK))
    shared(1)
    have_response(1)
    for b in range(RBLK):
        total = tail(1, b) + inverse(q_hi[b], q_lo[b])
        gated = (response(1, b).astype(F32) * total).astype(BF16)
        vs_ref[b] = spectrum(gated)
    shared(2)
    head_spectrum(2)
    response_products(range(RBLK))

    my_work = rows_of(yy, WORK)

    def out_copy(b, k):
        peer = y_peer(k)
        at = pl.ds(b * BLK, BLK)
        return pltpu.make_async_remote_copy(
            src_ref=out_send.at[peer, :, at],
            dst_ref=out_home.at[my_work, at],
            send_sem=out_send_sem.at[b, k],
            recv_sem=out_recv_sem.at[b, k],
            device_id={"ctx": zh * NY + peer},
            device_id_type=MESH,
        )

    for b in range(RBLK):
        at = slice(b * BLK, (b + 1) * BLK)
        own = inverse(q_hi[b], q_lo[b])
        loop(1, NZ, lambda k: last_copy(b, k).wait_recv())
        out_send[:, :, at] = (tail(3, b) + own).astype(BF16).reshape(NY, WORK, BLK)
        loop(1, NY, lambda k: out_copy(b, k).start())
        out_home[my_work, at] = out_send[yy, :, at]

    def back_copy(k):
        peer = ctx_peer(k)
        return pltpu.make_async_remote_copy(
            src_ref=back_send.at[rows_of(peer, OWN), :],
            dst_ref=back_recv.at[my_group, :],
            send_sem=back_send_sem.at[k],
            recv_sem=back_recv_sem.at[k],
            device_id={"ctx": peer},
            device_id_type=MESH,
        )

    loop(1, NCTX, lambda k: back_copy(k).start())
    back_recv[my_group, :] = back_send[mine, :]

    weight = jnp.broadcast_to(rd_ref[...], (16, BLK))
    w_hi = weight.astype(BF16).astype(F32)
    w_mid = (weight - w_hi).astype(BF16).astype(F32)
    w_lo = weight - w_hi - w_mid
    w_row = lax.broadcasted_iota(jnp.int32, (16, BLK), 0)
    weight = jnp.where(
        w_row == 0, w_hi, jnp.where(w_row == 1, w_mid, jnp.where(w_row == 2, w_lo, 0.0))
    ).astype(BF16)

    for b in range(RBLK):
        at = slice(b * BLK, (b + 1) * BLK)
        loop(1, NY, lambda k: out_copy(b, k).wait_recv())
        value = (resp_send[2, :, at].astype(F32) * out_home[:, at].astype(F32)).astype(BF16)
        resp_send[2, :, at] = value
        part = jnp.sum(dot(weight, value), axis=0, keepdims=True)
        p_send[2 * b : 2 * b + 1, :] = part[:, :128]
        p_send[2 * b + 1 : 2 * b + 2, :] = part[:, 128:]

    def p_copy(k):
        return pltpu.make_async_remote_copy(
            src_ref=p_send,
            dst_ref=p_recv.at[mc],
            send_sem=p_send_sem.at[k],
            recv_sem=p_recv_sem.at[k],
            device_id={"ch": lax.rem(mc + k, nch)},
            device_id_type=MESH,
        )

    if nch > 1:
        loop(1, nch, lambda k: p_copy(k).start())
    p_recv[mc] = p_send[...]

    length = len_ref[0]
    stores = []
    for b in range(RBLK):
        at = slice(b * BLK, (b + 1) * BLK)
        token = lax.broadcasted_iota(jnp.int32, (BLK, BLK), 0) + b * BLK
        value = jnp.transpose(resp_send[2, :, at].astype(F32))
        out_ref[at, :] = jnp.where(token < length, value, 0.0).astype(BF16)
        rows = pl.ds(b * BLK, BLK)
        stores.append(
            pltpu.make_async_copy(out_ref.at[rows, :], out_hbm.at[rows, :], store_sem.at[b])
        )
        stores[-1].start()
    loop(1, NCTX, lambda k: back_copy(k).wait_recv())
    po_ref[...] = (
        g2_ref[...].astype(F32) * jnp.transpose(back_recv[...].astype(F32))
    ).astype(BF16)
    stores.append(pltpu.make_async_copy(po_ref, po_hbm, store_sem.at[RBLK]))
    stores[-1].start()

    for stage in range(2):
        loop(1, NCTX, lambda k: in_copy(stage, k).wait_send())
    for which in range(2):
        loop(1, NY, lambda k: resp_copy(which, k).wait_send())
    for kind in range(3):
        loop(1, NZ, lambda k: gz_copy(kind, k).wait_send())
    for b in range(RBLK):
        loop(1, NZ, lambda k: last_copy(b, k).wait_send())
        loop(1, NY, lambda k: out_copy(b, k).wait_send())
    loop(1, NCTX, lambda k: back_copy(k).wait_send())

    if nch > 1:
        loop(1, nch, lambda k: p_copy(k).wait_recv())
    projection = p_recv[0]
    for c in range(1, nch):
        projection = projection + p_recv[c]
    token = (
        lax.broadcasted_iota(jnp.int32, (8, 128), 0) * 128
        + lax.broadcasted_iota(jnp.int32, (8, 128), 1)
    )
    squares = jnp.where(token < length, projection * projection, 0.0)
    sc_ref[0] = jnp.sum(squares) / length.astype(F32)
    if nch > 1:
        loop(1, nch, lambda k: p_copy(k).wait_send())
    for copy in stores:
        copy.wait()


def place(a_ref, b_ref, a_out, b_out, a_buf, b_buf, sem):
    pairs = [(a_ref, a_buf, a_out)]
    for b in range(RBLK):
        rows = pl.ds(b * BLK, BLK)
        pairs.append((b_ref.at[rows, :], b_buf.at[rows, :], b_out.at[rows, :]))
    loads, stores = [], []
    for n, (source, buffer, target) in enumerate(pairs):
        loads.append(pltpu.make_async_copy(source, buffer, sem.at[0, n]))
        stores.append(pltpu.make_async_copy(buffer, target, sem.at[1, n]))
    for copy in loads:
        copy.start()
    for load, store in zip(loads, stores):
        load.wait()
        store.start()
    for copy in stores:
        copy.wait()


def per_device(
    nch,
    prefix_values,
    inner_gate,
    outer_gate,
    inner_filter,
    outer_filter,
    response_values,
    response_inner,
    response_outer,
    lengths,
    readout,
):
    hbm = pl.BlockSpec(memory_space=pl.ANY)
    smem = pl.BlockSpec(memory_space=pltpu.SMEM)
    dma = pltpu.SemaphoreType.DMA
    tokens = RBLK * BLK
    prefix_output, response_output, scores = pl.pallas_call(
        functools.partial(kernel, nch),
        out_shape=(
            jax.ShapeDtypeStruct((BLK, BLK), BF16),
            jax.ShapeDtypeStruct((tokens, BLK), BF16),
            jax.ShapeDtypeStruct((1,), F32),
        ),
        in_specs=[hbm] * 8 + [smem] + [hbm] * 5,
        out_specs=(hbm, hbm, smem),
        scratch_shapes=[
            pltpu.VMEM((BLK, BLK), BF16),
            pltpu.VMEM((tokens, BLK), BF16),
            dma((RBLK + 1,)),
            *[pltpu.VMEM((BLK, BLK), BF16) for _ in range(5)],
            *[pltpu.VMEM((tokens, BLK), BF16) for _ in range(3)],
            pltpu.VMEM((1, BLK), F32),
            *[pltpu.VMEM((2 * BLK, BLK), BF16) for _ in range(2)],
            *[pltpu.VMEM((BLK, 2 * BLK), BF16) for _ in range(2)],
            dma((13,)),
            pltpu.VMEM((4, BLK, BLK), BF16),
            pltpu.VMEM((4, BLK, BLK), BF16),
            pltpu.VMEM((3, BLK, tokens), BF16),
            pltpu.VMEM((2, NY, WORK, tokens), BF16),
            pltpu.VMEM((NCTX + 1, OWN, BLK), F32),
            pltpu.VMEM((NCTX + 1, OWN, BLK), F32),
            pltpu.VMEM((NCTX, OWN, BLK), F32),
            pltpu.VMEM((NCTX, OWN, BLK), F32),
            pltpu.VMEM((NOUT * OWN, 2 * BLK), F32),
            pltpu.VMEM((4, RBLK, NZ, OWN, BLK), BF16),
            pltpu.VMEM((BLK, BLK), BF16),
            pltpu.VMEM((BLK, BLK), BF16),
            pltpu.VMEM((RBLK, BLK, 2 * BLK), F32),
            pltpu.VMEM((RBLK * WORK, 2 * BLK), F32),
            pltpu.VMEM((RBLK, BLK, 2 * BLK), BF16),
            pltpu.VMEM((RBLK, BLK, 2 * BLK), BF16),
            pltpu.VMEM((NY, WORK, tokens), BF16),
            pltpu.VMEM((BLK, tokens), BF16),
            pltpu.VMEM((8, 128), F32),
            pltpu.VMEM((nch, 8, 128), F32),
            dma((2, NCTX)),
            dma((2, NCTX)),
            dma((2, NY)),
            dma((2, NY)),
            dma((3, NZ)),
            dma((3, NZ)),
            dma((RBLK, NZ)),
            dma((RBLK, NZ)),
            dma((NCTX,)),
            dma((NCTX,)),
            dma((RBLK, NY)),
            dma((RBLK, NY)),
            dma((nch,)),
            dma((nch,)),
        ],
        compiler_params=pltpu.CompilerParams(
            collective_id=0, has_side_effects=True, vmem_limit_bytes=60 * 1024 * 1024
        ),
        cost_estimate=pl.CostEstimate(
            flops=8_000_000_000, bytes_accessed=5_000_000, transcendentals=0
        ),
        name="gated_convolutions",
    )(
        prefix_values,
        inner_gate,
        outer_gate,
        inner_filter,
        outer_filter,
        response_values.reshape(tokens, BLK),
        response_inner.reshape(tokens, BLK),
        response_outer.reshape(tokens, BLK),
        lengths,
        readout.reshape(1, BLK),
        *[jnp.asarray(t) for t in dft_tables()],
    )
    prefix_output, response_output = pl.pallas_call(
        place,
        out_shape=(
            jax.ShapeDtypeStruct((BLK, BLK), BF16),
            jax.ShapeDtypeStruct((tokens, BLK), BF16),
        ),
        in_specs=[hbm] * 2,
        out_specs=(hbm, hbm),
        scratch_shapes=[
            pltpu.VMEM((BLK, BLK), BF16),
            pltpu.VMEM((tokens, BLK), BF16),
            dma((2, RBLK + 1)),
        ],
        compiler_params=pltpu.CompilerParams(vmem_limit_bytes=60 * 1024 * 1024),
        name="place_outputs",
    )(prefix_output, response_output)
    return prefix_output, response_output.reshape(1, tokens, BLK), scores


def solution(mesh):
    in_specs = (
        P("ctx", "ch"),
        P("ctx", "ch"),
        P("ctx", "ch"),
        P("ctx", "ch"),
        P("ctx", "ch"),
        P("ctx", None, "ch"),
        P("ctx", None, "ch"),
        P("ctx", None, "ch"),
        P("ctx"),
        P("ch"),
    )
    out_specs = (P("ctx", "ch"), P("ctx", None, "ch"), P("ctx"))
    return jax.shard_map(
        functools.partial(per_device, mesh.shape["ch"]),
        mesh=mesh,
        in_specs=in_specs,
        out_specs=out_specs,
        check_vma=False,
    )
```

time: 83.6 us -> 59.6 us (0.71)
  local copies, waits for them, and re-layouts: 13.6 us -> 0 us
  Pallas kernels: 66.5 us -> 56.4 us
    unnamed x28 -> x0, local copies, waits for them, and re-layouts: 13.6 us -> none
    pallas_call x1, Pallas kernels: 66.5 us -> 54.5 us  [per_device(): pl.pallas_call(functools.partial(kernel, nch), out_shape=(jax.ShapeDtypeS...]
    pallas_call x0 -> x1, Pallas kernels: none -> 1.91 us  [per_device(): pl.pallas_call(place, out_shape=(jax.ShapeDtypeStruct((BLK, BLK), BF16),...]
where the time goes in v2:
time: 59.6 us; the launch traced here: 59.5 us
  Pallas kernels  56.4 us (95%)
  between operations  3.05 us (5%)
    pallas_call x1, Pallas kernels, per_device(): pl.pallas_call(functools.partial(kernel, nch), out_shape=(jax.ShapeDtypeS...  54.5 us
    pallas_call x1, Pallas kernels, per_device(): pl.pallas_call(place, out_shape=(jax.ShapeDtypeStruct((BLK, BLK), BF16),...  1.91 us

profile of v2, /device:TPU:1, one launch (start us, length us, event | category | flops | bytes accessed | tf_op | source)
XLA Modules:
  0.0 59.5 jit_solution(8690737765601188080)
XLA Ops:
  1.3 54.5 %gated_convolutions.1 = (bf16[256,256]{1,0:T(8,128)(2,1)}, bf16[1024,256]{1,0:T(8,128)(2,1)}, f32[1]{0:T(128)}) custom-call(bf16[256,256]{1,0:T(8,128)(2,1)} %x_hbm.1, bf16[256,256]{1,0:T(8,128)(2,1)} %g1_hbm.1, bf16[256,256]{1,0:T(8,128)(2,1)} %g2_hbm.1, bf16[256,256]{1,0:T(8,128)(2,1)} %h1_hbm.1, bf16[256,256]{1,0:T(8,128)(2,1)} %h2_hbm.1, ...), custom_call_target="tpu_custom_call" | custom-call | flops 8000000000 | bytes 5000000 | tf_op jit(solution)/shard_map/gated_convolutions/pallas_call | solution.py:542
  55.8 1.9 %place_outputs.1 = (bf16[256,256]{1,0:T(8,128)(2,1)}, bf16[1024,256]{1,0:T(8,128)(2,1)}) custom-call(bf16[256,256]{1,0:T(8,128)(2,1)} %get-tuple-element.8.a_ref, bf16[1024,256]{1,0:T(8,128)(2,1)} %get-tuple-element.9.b_ref), custom_call_target="tpu_custom_call" | custom-call | tf_op jit(solution)/shard_map/place_outputs/pallas_call | solution.py:616

commit v3 on v2

--- a/solution.py
+++ b/solution.py
@@ -96,6 +96,8 @@
     q_lo,
     out_send,
     out_home,
+    part_send,
+    part_recv,
     p_send,
     p_recv,
     in_send_sem,
@@ -110,6 +112,8 @@
     back_recv_sem,
     out_send_sem,
     out_recv_sem,
+    part_send_sem,
+    part_recv_sem,
     p_send_sem,
     p_recv_sem,
 ):
@@ -209,14 +213,11 @@
             device_id_type=MESH,
         )
 
-    def turn(which, ref):
+    def send_response(which, ref):
         loaded(ref)
         for b in range(RBLK):
             at = slice(b * BLK, (b + 1) * BLK)
             resp_send[which, :, at] = jnp.transpose(ref[at, :])
-
-    def send_response(which, ref):
-        turn(which, ref)
         loop(1, NY, lambda k: resp_copy(which, k).start())
         resp_recv[which, yy] = resp_send[which, rows_of(yy, WORK), :]
 
@@ -355,7 +356,7 @@
     loop(1, NCTX, lambda k: in_copy(1, k).start())
     send_response(0, v_ref)
     send_response(1, ri_ref)
-    turn(2, ro_ref)
+    send_response(2, ro_ref)
     loaded(ft_hi, ft_lo, f_hi, f_lo, g2_ref, rd_ref)
 
     loop(1, NCTX, lambda k: in_copy(0, k).wait_recv())
@@ -388,6 +389,20 @@
     shared(2)
     head_spectrum(2)
     response_products(range(RBLK))
+    have_response(2)
+
+    lane = lax.broadcasted_iota(jnp.int32, (16, BLK), 1)
+    row = lax.broadcasted_iota(jnp.int32, (16, BLK), 0)
+    weight = jnp.where(lane // WORK == yy, jnp.broadcast_to(rd_ref[...], (16, BLK)), 0.0)
+    weight = weight + pltpu.roll(weight, BLK // 2, 1)
+    weight = weight + pltpu.roll(weight, WORK, 1)
+    w_hi = weight.astype(BF16).astype(F32)
+    w_mid = (weight - w_hi).astype(BF16).astype(F32)
+    w_lo = weight - w_hi - w_mid
+    term = row // NY
+    weight = jnp.where(term == 0, w_hi, jnp.where(term == 1, w_mid, w_lo))
+    weight = jnp.where(term < 3, weight, 0.0)
+    weight = jnp.where(lax.rem(row, NY) == lane // WORK, weight, 0.0).astype(BF16)
 
     my_work = rows_of(yy, WORK)
 
@@ -404,12 +419,52 @@
         )
 
     for b in range(RBLK):
+        vs_ref[b, :, :BLK] = inverse(q_hi[b], q_lo[b])
+
+    for b in range(RBLK):
         at = slice(b * BLK, (b + 1) * BLK)
-        own = inverse(q_hi[b], q_lo[b])
         loop(1, NZ, lambda k: last_copy(b, k).wait_recv())
-        out_send[:, :, at] = (tail(3, b) + own).astype(BF16).reshape(NY, WORK, BLK)
+        total = tail(3, b) + vs_ref[b, :, :BLK]
+        value = (response(2, b).astype(F32) * total).astype(BF16)
+        out_send[:, :, at] = value.reshape(NY, WORK, BLK)
+        terms = dot(weight, value)
+        part = terms[0:4] + terms[4:8] + terms[8:12]
+        for n in range(NY):
+            part_send[n, 2 * b : 2 * b + 1, :] = part[n : n + 1, :128]
+            part_send[n, 2 * b + 1 : 2 * b + 2, :] = part[n : n + 1, 128:]
+
+    def part_copy(k):
+        peer = y_peer(k)
+        return pltpu.make_async_remote_copy(
+            src_ref=part_send.at[peer],
+            dst_ref=part_recv.at[yy],
+            send_sem=part_send_sem.at[k],
+            recv_sem=part_recv_sem.at[k],
+            device_id={"ctx": zh * NY + peer},
+            device_id_type=MESH,
+        )
+
+    loop(1, NY, lambda k: part_copy(k).start())
+    for b in range(RBLK):
         loop(1, NY, lambda k: out_copy(b, k).start())
-        out_home[my_work, at] = out_send[yy, :, at]
+    part_recv[yy] = part_send[yy]
+    out_home[my_work, :] = out_send[yy]
+
+    def p_copy(k):
+        return pltpu.make_async_remote_copy(
+            src_ref=p_send,
+            dst_ref=p_recv.at[mc],
+            send_sem=p_send_sem.at[k],
+            recv_sem=p_recv_sem.at[k],
+            device_id={"ch": lax.rem(mc + k, nch)},
+            device_id_type=MESH,
+        )
+
+    loop(1, NY, lambda k: part_copy(k).wait_recv())
+    p_send[...] = part_recv[0] + part_recv[1] + part_recv[2] + part_recv[3]
+    if nch > 1:
+        loop(1, nch, lambda k: p_copy(k).start())
+    p_recv[mc] = p_send[...]
 
     def back_copy(k):
         peer = ctx_peer(k)
@@ -425,44 +480,13 @@
     loop(1, NCTX, lambda k: back_copy(k).start())
     back_recv[my_group, :] = back_send[mine, :]
 
-    weight = jnp.broadcast_to(rd_ref[...], (16, BLK))
-    w_hi = weight.astype(BF16).astype(F32)
-    w_mid = (weight - w_hi).astype(BF16).astype(F32)
-    w_lo = weight - w_hi - w_mid
-    w_row = lax.broadcasted_iota(jnp.int32, (16, BLK), 0)
-    weight = jnp.where(
-        w_row == 0, w_hi, jnp.where(w_row == 1, w_mid, jnp.where(w_row == 2, w_lo, 0.0))
-    ).astype(BF16)
-
+    length = len_ref[0]
+    stores = []
     for b in range(RBLK):
         at = slice(b * BLK, (b + 1) * BLK)
         loop(1, NY, lambda k: out_copy(b, k).wait_recv())
-        value = (resp_send[2, :, at].astype(F32) * out_home[:, at].astype(F32)).astype(BF16)
-        resp_send[2, :, at] = value
-        part = jnp.sum(dot(weight, value), axis=0, keepdims=True)
-        p_send[2 * b : 2 * b + 1, :] = part[:, :128]
-        p_send[2 * b + 1 : 2 * b + 2, :] = part[:, 128:]
-
-    def p_copy(k):
-        return pltpu.make_async_remote_copy(
-            src_ref=p_send,
-            dst_ref=p_recv.at[mc],
-            send_sem=p_send_sem.at[k],
-            recv_sem=p_recv_sem.at[k],
-            device_id={"ch": lax.rem(mc + k, nch)},
-            device_id_type=MESH,
-        )
-
-    if nch > 1:
-        loop(1, nch, lambda k: p_copy(k).start())
-    p_recv[mc] = p_send[...]
-
-    length = len_ref[0]
-    stores = []
-    for b in range(RBLK):
-        at = slice(b * BLK, (b + 1) * BLK)
         token = lax.broadcasted_iota(jnp.int32, (BLK, BLK), 0) + b * BLK
-        value = jnp.transpose(resp_send[2, :, at].astype(F32))
+        value = jnp.transpose(out_home[:, at].astype(F32))
         out_ref[at, :] = jnp.where(token < length, value, 0.0).astype(BF16)
         rows = pl.ds(b * BLK, BLK)
         stores.append(
@@ -478,7 +502,7 @@
 
     for stage in range(2):
         loop(1, NCTX, lambda k: in_copy(stage, k).wait_send())
-    for which in range(2):
+    for which in range(3):
         loop(1, NY, lambda k: resp_copy(which, k).wait_send())
     for kind in range(3):
         loop(1, NZ, lambda k: gz_copy(kind, k).wait_send())
@@ -486,6 +510,7 @@
         loop(1, NZ, lambda k: last_copy(b, k).wait_send())
         loop(1, NY, lambda k: out_copy(b, k).wait_send())
     loop(1, NCTX, lambda k: back_copy(k).wait_send())
+    loop(1, NY, lambda k: part_copy(k).wait_send())
 
     if nch > 1:
         loop(1, nch, lambda k: p_copy(k).wait_recv())
@@ -561,7 +586,7 @@
             pltpu.VMEM((4, BLK, BLK), BF16),
             pltpu.VMEM((4, BLK, BLK), BF16),
             pltpu.VMEM((3, BLK, tokens), BF16),
-            pltpu.VMEM((2, NY, WORK, tokens), BF16),
+            pltpu.VMEM((3, NY, WORK, tokens), BF16),
             pltpu.VMEM((NCTX + 1, OWN, BLK), F32),
             pltpu.VMEM((NCTX + 1, OWN, BLK), F32),
             pltpu.VMEM((NCTX, OWN, BLK), F32),
@@ -576,12 +601,14 @@
             pltpu.VMEM((RBLK, BLK, 2 * BLK), BF16),
             pltpu.VMEM((NY, WORK, tokens), BF16),
             pltpu.VMEM((BLK, tokens), BF16),
+            pltpu.VMEM((NY, 8, 128), F32),
+            pltpu.VMEM((NY, 8, 128), F32),
             pltpu.VMEM((8, 128), F32),
             pltpu.VMEM((nch, 8, 128), F32),
             dma((2, NCTX)),
             dma((2, NCTX)),
-            dma((2, NY)),
-            dma((2, NY)),
+            dma((3, NY)),
+            dma((3, NY)),
             dma((3, NZ)),
             dma((3, NZ)),
             dma((RBLK, NZ)),
@@ -590,6 +617,8 @@
             dma((NCTX,)),
             dma((RBLK, NY)),
             dma((RBLK, NY)),
+            dma((NY,)),
+            dma((NY,)),
             dma((nch,)),
             dma((nch,)),
         ],

time: 59.6 us -> 57.9 us (0.971)
  Pallas kernels: 56.4 us -> 54.7 us
    pallas_call x1, Pallas kernels: 54.5 us -> 52.8 us  [per_device(): pl.pallas_call(functools.partial(kernel, nch), out_shape=(jax.ShapeDtypeS...]
where the time goes in v3:
time: 57.9 us; the launch traced here: 57.7 us
  Pallas kernels  54.7 us (94%)
  between operations  3.05 us (5%)
    pallas_call x1, Pallas kernels, per_device(): pl.pallas_call(functools.partial(kernel, nch), out_shape=(jax.ShapeDtypeS...  52.8 us
    pallas_call x1, Pallas kernels, per_device(): pl.pallas_call(place, out_shape=(jax.ShapeDtypeStruct((BLK, BLK), BF16),...  1.91 us

profile of v3, /device:TPU:1, one launch (start us, length us, event | category | flops | bytes accessed | tf_op | source)
XLA Modules:
  0.0 57.7 jit_solution(8796162750366250887)
XLA Ops:
  1.3 52.8 %gated_convolutions.1 = (bf16[256,256]{1,0:T(8,128)(2,1)}, bf16[1024,256]{1,0:T(8,128)(2,1)}, f32[1]{0:T(128)}) custom-call(bf16[256,256]{1,0:T(8,128)(2,1)} %x_hbm.1, bf16[256,256]{1,0:T(8,128)(2,1)} %g1_hbm.1, bf16[256,256]{1,0:T(8,128)(2,1)} %g2_hbm.1, bf16[256,256]{1,0:T(8,128)(2,1)} %h1_hbm.1, bf16[256,256]{1,0:T(8,128)(2,1)} %h2_hbm.1, ...), custom_call_target="tpu_custom_call" | custom-call | flops 8000000000 | bytes 5000000 | tf_op jit(solution)/shard_map/gated_convolutions/pallas_call | solution.py:567
  54.1 1.9 %place_outputs.1 = (bf16[256,256]{1,0:T(8,128)(2,1)}, bf16[1024,256]{1,0:T(8,128)(2,1)}) custom-call(bf16[256,256]{1,0:T(8,128)(2,1)} %get-tuple-element.8.a_ref, bf16[1024,256]{1,0:T(8,128)(2,1)} %get-tuple-element.9.b_ref), custom_call_target="tpu_custom_call" | custom-call | tf_op jit(solution)/shard_map/place_outputs/pallas_call | solution.py:645

commit v4 on v3

--- a/solution.py
+++ b/solution.py
@@ -106,8 +106,6 @@
     resp_recv_sem,
     gz_send_sem,
     gz_recv_sem,
-    last_send_sem,
-    last_recv_sem,
     back_send_sem,
     back_recv_sem,
     out_send_sem,
@@ -241,17 +239,6 @@
             device_id_type=MESH,
         )
 
-    def last_copy(b, k):
-        part = gath.at[3, b, zh]
-        return pltpu.make_async_remote_copy(
-            src_ref=part,
-            dst_ref=part,
-            send_sem=last_send_sem.at[b, k],
-            recv_sem=last_recv_sem.at[b, k],
-            device_id={"ctx": z_index(k) * NY + yy},
-            device_id_type=MESH,
-        )
-
     def store_rows(kind, rows):
         for b in range(RBLK):
             gath[kind, b, zh] = rows[b * OWN : (b + 1) * OWN]
@@ -262,11 +249,6 @@
 
     def shared(kind):
         loop(1, NZ, lambda k: gz_copy(kind, k).wait_recv())
-
-    def share_last(rows):
-        store_rows(3, rows)
-        for b in range(RBLK):
-            loop(1, NZ, lambda k: last_copy(b, k).start())
 
     def tail(kind, b):
         rows = gath[kind, b].astype(F32).reshape(WORK, BLK)
@@ -374,7 +356,7 @@
     set_taps(recv_in[3])
     gated = (recv_in[2].astype(F32) * conv[:BLK]).astype(BF16)
     conv = owner_convolution(gated)
-    share_last(conv[BLK:].astype(BF16))
+    share(3, conv[BLK:].astype(BF16))
     back_send[...] = conv[:BLK].astype(BF16)
 
     shared(0)
@@ -405,10 +387,11 @@
     weight = jnp.where(lax.rem(row, NY) == lane // WORK, weight, 0.0).astype(BF16)
 
     my_work = rows_of(yy, WORK)
+    half = RBLK * BLK // 2
 
     def out_copy(b, k):
         peer = y_peer(k)
-        at = pl.ds(b * BLK, BLK)
+        at = pl.ds(b * half, half)
         return pltpu.make_async_remote_copy(
             src_ref=out_send.at[peer, :, at],
             dst_ref=out_home.at[my_work, at],
@@ -420,10 +403,10 @@
 
     for b in range(RBLK):
         vs_ref[b, :, :BLK] = inverse(q_hi[b], q_lo[b])
+    shared(3)
 
     for b in range(RBLK):
         at = slice(b * BLK, (b + 1) * BLK)
-        loop(1, NZ, lambda k: last_copy(b, k).wait_recv())
         total = tail(3, b) + vs_ref[b, :, :BLK]
         value = (response(2, b).astype(F32) * total).astype(BF16)
         out_send[:, :, at] = value.reshape(NY, WORK, BLK)
@@ -445,7 +428,7 @@
         )
 
     loop(1, NY, lambda k: part_copy(k).start())
-    for b in range(RBLK):
+    for b in range(2):
         loop(1, NY, lambda k: out_copy(b, k).start())
     part_recv[yy] = part_send[yy]
     out_home[my_work, :] = out_send[yy]
@@ -484,7 +467,8 @@
     stores = []
     for b in range(RBLK):
         at = slice(b * BLK, (b + 1) * BLK)
-        loop(1, NY, lambda k: out_copy(b, k).wait_recv())
+        if b % 2 == 0:
+            loop(1, NY, lambda k: out_copy(b // 2, k).wait_recv())
         token = lax.broadcasted_iota(jnp.int32, (BLK, BLK), 0) + b * BLK
         value = jnp.transpose(out_home[:, at].astype(F32))
         out_ref[at, :] = jnp.where(token < length, value, 0.0).astype(BF16)
@@ -504,10 +488,9 @@
         loop(1, NCTX, lambda k: in_copy(stage, k).wait_send())
     for which in range(3):
         loop(1, NY, lambda k: resp_copy(which, k).wait_send())
-    for kind in range(3):
+    for kind in range(4):
         loop(1, NZ, lambda k: gz_copy(kind, k).wait_send())
-    for b in range(RBLK):
-        loop(1, NZ, lambda k: last_copy(b, k).wait_send())
+    for b in range(2):
         loop(1, NY, lambda k: out_copy(b, k).wait_send())
     loop(1, NCTX, lambda k: back_copy(k).wait_send())
     loop(1, NY, lambda k: part_copy(k).wait_send())
@@ -609,14 +592,12 @@
             dma((2, NCTX)),
             dma((3, NY)),
             dma((3, NY)),
-            dma((3, NZ)),
-            dma((3, NZ)),
-            dma((RBLK, NZ)),
-            dma((RBLK, NZ)),
+            dma((4, NZ)),
+            dma((4, NZ)),
             dma((NCTX,)),
             dma((NCTX,)),
-            dma((RBLK, NY)),
-            dma((RBLK, NY)),
+            dma((2, NY)),
+            dma((2, NY)),
             dma((NY,)),
             dma((NY,)),
             dma((nch,)),

time: 57.9 us -> 57.3 us (0.990)
  Pallas kernels: 54.7 us -> 54.1 us
    pallas_call x1, Pallas kernels: 52.8 us -> 52.2 us  [per_device(): pl.pallas_call(functools.partial(kernel, nch), out_shape=(jax.ShapeDtypeS...]
where the time goes in v4:
time: 57.3 us; the launch traced here: 57.1 us
  Pallas kernels  54.1 us (94%)
  between operations  3.05 us (5%)
    pallas_call x1, Pallas kernels, per_device(): pl.pallas_call(functools.partial(kernel, nch), out_shape=(jax.ShapeDtypeS...  52.2 us
    pallas_call x1, Pallas kernels, per_device(): pl.pallas_call(place, out_shape=(jax.ShapeDtypeStruct((BLK, BLK), BF16),...  1.91 us

profile of v4, /device:TPU:1, one launch (start us, length us, event | category | flops | bytes accessed | tf_op | source)
XLA Modules:
  0.0 57.1 jit_solution(6456413299238652247)
XLA Ops:
  1.3 52.2 %gated_convolutions.1 = (bf16[256,256]{1,0:T(8,128)(2,1)}, bf16[1024,256]{1,0:T(8,128)(2,1)}, f32[1]{0:T(128)}) custom-call(bf16[256,256]{1,0:T(8,128)(2,1)} %x_hbm.1, bf16[256,256]{1,0:T(8,128)(2,1)} %g1_hbm.1, bf16[256,256]{1,0:T(8,128)(2,1)} %g2_hbm.1, bf16[256,256]{1,0:T(8,128)(2,1)} %h1_hbm.1, bf16[256,256]{1,0:T(8,128)(2,1)} %h2_hbm.1, ...), custom_call_target="tpu_custom_call" | custom-call | flops 8000000000 | bytes 5000000 | tf_op jit(solution)/shard_map/gated_convolutions/pallas_call | solution.py:550
  53.5 1.9 %place_outputs.1 = (bf16[256,256]{1,0:T(8,128)(2,1)}, bf16[1024,256]{1,0:T(8,128)(2,1)}) custom-call(bf16[256,256]{1,0:T(8,128)(2,1)} %get-tuple-element.8.a_ref, bf16[1024,256]{1,0:T(8,128)(2,1)} %get-tuple-element.9.b_ref), custom_call_target="tpu_custom_call" | custom-call | tf_op jit(solution)/shard_map/place_outputs/pallas_call | solution.py:626
